TPU v7x, 1024 devices: a whole 4x8x16 slice. The times are simulated.
1024 devices in a mesh: dp: 16 (over z), expert: 64 (over x, y, core).
Axes of the slice: x: 4, y: 8, z: 16, core: 2. Of those that a mesh axis runs over, the one named last changes fastest.
Arguments:
- tokens: bfloat16 [2048, 4096], P('expert', 'dp'), may hold values from -6 to 6
- routes: int32 [2048, 8], P('expert'), may hold values from 0 to 63, all different within a row; in each aligned block of 32 rows (0 to 31, 32 to 63, ...) at most 8 rows name the same one
- gates: float32 [2048, 8], P('expert'), may hold values from 0.1 to 1
- counts: int32 [64], replicated, may hold values from 1 to 8
- w_gate_up: bfloat16 [64, 4096, 2, 1024], P('expert', 'dp'), may hold values from -0.09375 to 0.09375
- w_down: bfloat16 [64, 4096, 1024], P('expert', 'dp'), may hold values from -0.1875 to 0.1875
- cotangent: bfloat16 [2048, 4096], P('expert', 'dp'), may hold values from -6 to 6
Outputs:
- mixed: bfloat16 [2048, 4096], P('expert', 'dp')
- gate_grad: float32 [2048, 8], P('expert')
- token_grad: bfloat16 [2048, 4096], P('expert', 'dp')
- weight_grads: bfloat16 [64, 4096, 3, 1024], P('expert', 'dp')
Inputs may be any that keep to these rules, and one draw needn't show every extreme that they name: `routes`: each token names 8 different experts; within the tokens of one group (32 tokens in a row from the start) no expert is named more than 8 times, a bound that some block reaches.
All inputs are finite; a program needn't handle non-finite values.
Results may differ from a plain program's by a relative error of at most 0.0064.
Values may be sent and summed in bfloat16 or wider, within the bound.
No kernel may reach another device: no remote copies, remote signals or barrier semaphores. Data moves between devices by JAX's collectives and lax.ppermute only.
A program may use at most 32 MiB of HBM per device.

v0:
```python
import jax
import jax.numpy as jnp
from jax import lax
from jax.sharding import PartitionSpec as P


def shards(tokens, routes, gates, counts, w_gate_up, w_down, cotangent):
    experts = lax.axis_size("expert")
    tok_rows, slice_width = tokens.shape
    route_count = routes.shape[1]
    capacity = min(tok_rows, 2 * tok_rows * route_count // experts)
    slot_total = experts * capacity
    flat_routes = routes.reshape(-1)
    member = (flat_routes[:, None] == jnp.arange(experts, dtype=jnp.int32)[None, :]).astype(
        jnp.int32
    )
    before = jnp.sum((jnp.cumsum(member, axis=0) - 1) * member, axis=1)
    target = flat_routes * capacity + before
    placing = (jnp.arange(slot_total, dtype=jnp.int32)[:, None] == target[None, :]).astype(
        jnp.bfloat16
    )
    per_token = jnp.sum(placing.reshape(slot_total, tok_rows, route_count), axis=2)
    outgoing = (
        jnp.dot(per_token, tokens, preferred_element_type=jnp.float32)
        .astype(jnp.bfloat16)
        .reshape(experts, capacity, slice_width)
    )
    scaled = (
        (gates[:, :, None] * cotangent[:, None, :].astype(jnp.float32))
        .astype(jnp.bfloat16)
        .reshape(tok_rows * route_count, slice_width)
    )
    grad_out = (
        jnp.dot(placing, scaled, preferred_element_type=jnp.float32)
        .astype(jnp.bfloat16)
        .reshape(experts, capacity, slice_width)
    )
    arrived = lax.all_to_all(outgoing, "expert", split_axis=0, concat_axis=0, tiled=True)
    rows_in = arrived.reshape(slot_total, slice_width)
    pair_weight = w_gate_up[0]
    down_weight = w_down[0]
    partial_value = jnp.einsum(
        "nk,kcf->ncf", rows_in, pair_weight, preferred_element_type=jnp.float32
    )
    gate_up = lax.psum_scatter(partial_value, "dp", scatter_dimension=2, tiled=True)
    gate_part = gate_up[:, 0, :]
    up_part = gate_up[:, 1, :]
    sig_gate = jax.nn.sigmoid(gate_part)
    silu_gate = gate_part * sig_gate
    hidden_part = (silu_gate * up_part).astype(jnp.bfloat16)
    hidden_full = lax.all_gather(hidden_part, "dp", axis=1, tiled=True)
    expert_out = lax.dot_general(
        hidden_full, down_weight, (((1,), (1,)), ((), ())), preferred_element_type=jnp.float32
    ).astype(jnp.bfloat16)
    returned = lax.all_to_all(
        expert_out.reshape(experts, capacity, slice_width),
        "expert",
        split_axis=0,
        concat_axis=0,
        tiled=True,
    )
    route_out = lax.dot_general(
        placing,
        returned.reshape(slot_total, slice_width),
        (((0,), (0,)), ((), ())),
        preferred_element_type=jnp.float32,
    ).reshape(tok_rows, route_count, slice_width)
    mixed = jnp.sum(gates[:, :, None] * route_out, axis=1).astype(jnp.bfloat16)
    incoming = cotangent[:, None, :].astype(jnp.float32)
    gate_grad = lax.psum(jnp.sum(route_out * incoming, axis=2), "dp")
    grad_arrived = lax.all_to_all(grad_out, "expert", split_axis=0, concat_axis=0, tiled=True)
    grad_rows = grad_arrived.reshape(slot_total, slice_width)
    hidden_partial = jnp.dot(grad_rows, down_weight, preferred_element_type=jnp.float32)
    hidden_grad = lax.psum_scatter(hidden_partial, "dp", scatter_dimension=1, tiled=True)
    slope_term = sig_gate * (1.0 + gate_part * (1.0 - sig_gate))
    pair_grad = jnp.stack(
        [hidden_grad * up_part * slope_term, hidden_grad * silu_gate], axis=1
    ).astype(jnp.bfloat16)
    pair_full = lax.all_gather(pair_grad, "dp", axis=2, tiled=True)
    row_grad = jnp.einsum(
        "ncf,kcf->nk", pair_full, pair_weight, preferred_element_type=jnp.float32
    ).astype(jnp.bfloat16)
    returned_grad = lax.all_to_all(
        row_grad.reshape(experts, capacity, slice_width),
        "expert",
        split_axis=0,
        concat_axis=0,
        tiled=True,
    )
    token_grad = lax.dot_general(
        per_token,
        returned_grad.reshape(slot_total, slice_width),
        (((0,), (0,)), ((), ())),
        preferred_element_type=jnp.float32,
    ).astype(jnp.bfloat16)
    shares = counts.astype(jnp.float32) / jnp.sum(counts.astype(jnp.float32))
    slot_share = jnp.repeat(shares, capacity)
    weighted_pair = (slot_share[:, None, None] * pair_full.astype(jnp.float32)).astype(jnp.bfloat16)
    weighted_hidden = (slot_share[:, None] * hidden_full.astype(jnp.float32)).astype(jnp.bfloat16)
    pair_update = jnp.einsum(
        "nk,ncf->kcf", rows_in, weighted_pair, preferred_element_type=jnp.float32
    )
    down_update = lax.dot_general(
        grad_rows, weighted_hidden, (((0,), (0,)), ((), ())), preferred_element_type=jnp.float32
    )
    weight_grads = jnp.concatenate([pair_update, down_update[:, None, :]], axis=1).astype(
        jnp.bfloat16
    )
    return (mixed, gate_grad, token_grad, weight_grads[None])


def solution(mesh):
    return jax.shard_map(
        shards,
        mesh=mesh,
        in_specs=(
            P("expert", "dp"),
            P("expert", None),
            P("expert", None),
            P(),
            P("expert", "dp", None, None),
            P("expert", "dp", None),
            P("expert", "dp"),
        ),
        out_specs=(
            P("expert", "dp"),
            P("expert", None),
            P("expert", "dp"),
            P("expert", "dp", None, None),
        ),
        check_vma=False,
    )
```

profile of v0, /device:TPU:6, one launch (start us, length us, event | category | flops | bytes accessed | tf_op | source)
XLA Modules:
  0.0 433.6 jit_solution(2599471931227078872)
XLA Ops:
  7.2 0.8 copy.39
  8.2 0.7 convert_element_type.72
  9.0 0.8 copy.38
  9.7 0.6 reduce-window.6
  10.4 0.2 slice_reduce_fusion
  10.6 0.1 fusion.37
  10.8 0.3 fusion.6
  11.1 28.2 %all_to_all.20 = bf16[64,8,256]{2,1,0:T(8,128)(2,1)S(1)} all-to-all(bf16[64,8,256]{2,1,0:T(8,128)(2,1)S(1)} %fusion.6), channel_id=1, replica_groups=mesh['dp'=16,'expert'=64] {'expert'}, dimensions={0} | all-to-all | bytes 524288 | tf_op jit(solution)/shard_map/all_to_all | solution.py:71
  39.4 2.9 fusion.14
  42.4 0.2 fusion.21
  42.7 0.2 fusion.9
  42.9 17.8 %all_to_all.21 = bf16[64,8,256]{2,1,0:T(8,128)(2,1)S(1)} all-to-all(bf16[64,8,256]{2,1,0:T(8,128)(2,1)S(1)} %fusion.9), channel_id=1, replica_groups=mesh['dp'=16,'expert'=64] {'expert'}, dimensions={0} | all-to-all | bytes 524288 | tf_op jit(solution)/shard_map/all_to_all | solution.py:38
  60.7 2.7 fusion.11
  63.5 53.4 %reduce-scatter.5.cloned.1.call-done = f32[512,64]{0,1:T(8,128)} async-done(((f32[512,1024]{0,1:T(8,128)}), f32[512,64]{0,1:T(8,128)}) %reduce-scatter.5.cloned.1.call-update) | async-done | bytes 131088 | tf_op jit(solution)/shard_map/reduce_scatter | solution.py:74
  116.9 84.2 %reduce-scatter.3.cloned.1.call-done = f32[512,2,64]{0,2,1:T(8,128)} async-done(((f32[512,2,1024]{0,2,1:T(8,128)}), f32[512,2,64]{0,2,1:T(8,128)}) %reduce-scatter.3.cloned.1.call-update) | async-done | bytes 262160 | tf_op jit(solution)/shard_map/reduce_scatter | solution.py:45
  201.1 1.7 fusion.39
  202.9 0.7 pad_maximum_fusion.1
  203.6 0.6 convert_reduce_fusion
  204.2 72.1 %all-gather.3.cloned.1.call-done = bf16[512,1024]{0,1:T(8,128)(2,1)} async-done(((bf16[512,64]{0,1:T(8,128)(2,1)}), bf16[512,1024]{0,1:T(8,128)(2,1)}) %all-gather.3.cloned.1.call-update) | async-done | bytes 1048592 | tf_op jit(solution)/shard_map/all_gather | solution.py:51
  276.4 2.5 fusion.8
  278.9 10.5 %all-to-all-start.1 = ((bf16[64,8,256]{2,1,0:T(8,128)(2,1)}), bf16[64,8,256]{2,1,0:T(8,128)(2,1)S(1)}, u32[]{:S(2)}, u32[]{:S(2)}) async-start(bf16[64,8,256]{2,1,0:T(8,128)(2,1)} %fusion.8), calls=%async_computation.2 | async-start | bytes 524288 | tf_op jit(solution)/shard_map/all_to_all | solution.py:55
  289.4 0.7 convert_divide_fusion
  290.2 0.5 fusion.4
  290.7 61.8 %all-gather.5.cloned.1.call-done = bf16[512,2,1024]{0,2,1:T(8,128)(2,1)} async-done(((bf16[512,2,64]{0,2,1:T(8,128)(2,1)}), bf16[512,2,1024]{0,2,1:T(8,128)(2,1)}) %all-gather.5.cloned.1.call-update) | async-done | bytes 2097168 | tf_op jit(solution)/shard_map/all_gather | solution.py:79
  352.6 3.1 fusion.7
  355.7 10.5 %all-to-all-start.3 = ((bf16[64,8,256]{2,1,0:T(8,128)(2,1)}), bf16[64,8,256]{2,1,0:T(8,128)(2,1)S(1)}, u32[]{:S(2)}, u32[]{:S(2)}) async-start(bf16[64,8,256]{2,1,0:T(8,128)(2,1)} %fusion.7), calls=%async_computation.5 | async-start | bytes 524288 | tf_op jit(solution)/shard_map/all_to_all | solution.py:83
  366.1 0.9 multiply_reduce_fusion
  367.0 54.9 %psum.7 = f32[32,8]{1,0:T(8,128)S(1)} all-reduce(f32[32,8]{1,0:T(8,128)S(1)} %get-tuple-element.12), channel_id=1, replica_groups=mesh['dp'=16,'expert'=64] {'dp'}, use_global_device_ids=true, to_apply=%region_7.8 | all-reduce | flops 256 | bytes 2048 | tf_op jit(solution)/shard_map/psum | solution.py:70
  422.0 0.7 copy.48
  422.6 2.4 fusion.3
  425.0 1.3 pad_maximum_fusion
  426.3 0.8 convolution_convert_fusion.4
  (31 shorter events, 0.8 us)
Async XLA Ops:
  7.2 53.6 %copy-start = (bf16[1,256,2,1024]{3,2,1,0:T(2,128)(2,1)S(1)}, bf16[1,256,2,1024]{3,2,1,0:T(2,128)(2,1)}, u32[]{:S(2)}) copy-start(bf16[1,256,2,1024]{3,2,1,0:T(2,128)(2,1)} %param.11) | copy-start | bytes 3145732
  7.2 109.7 %reduce-scatter.5.cloned.1.call-start = ((), (), s32[]{:S(2)}) async-start(), calls=%async_computation.8 | async-start | bytes 2228224 | tf_op jit(solution)/shard_map/reduce_scatter | solution.py:74
  39.4 3.3 copy-start.2
  42.3 158.9 %reduce-scatter.3.cloned.1.call-start = ((), (), s32[]{:S(2)}) async-start(), calls=%async_computation.6 | async-start | bytes 4456448 | tf_op jit(solution)/shard_map/reduce_scatter | solution.py:45
  63.4 140.2 %copy-start.4 = (s32[64]{0:T(128)S(1)}, s32[64]{0:T(128)}, u32[]{:S(2)}) copy-start(s32[64]{0:T(128)} %param.10) | copy-start | bytes 772
  63.4 213.0 %copy-start.1 = (bf16[1,256,1024]{2,1,0:T(8,128)(2,1)S(1)}, bf16[1,256,1024]{2,1,0:T(8,128)(2,1)}, u32[]{:S(2)}) copy-start(bf16[1,256,1024]{2,1,0:T(8,128)(2,1)} %param.12) | copy-start | bytes 1572868
  63.5 212.9 %all-gather.3.cloned.1.call-start = ((), (), s32[]{:S(2)}) async-start(), calls=%async_computation.7 | async-start | bytes 1114112 | tf_op jit(solution)/shard_map/all_gather | solution.py:51
  202.9 149.7 %all-gather.5.cloned.1.call-start = ((), (), s32[]{:S(2)}) async-start(), calls=%async_computation.9 | async-start | bytes 2228224 | tf_op jit(solution)/shard_map/all_gather | solution.py:79
  276.4 13.8 %copy-start.3 = (bf16[512,1024]{0,1:T(8,128)(2,1)S(1)}, bf16[512,1024]{0,1:T(8,128)(2,1)}, u32[]{:S(2)}) copy-start(bf16[512,1024]{0,1:T(8,128)(2,1)} %all-gather.3.cloned.1.call-done) | copy-start | bytes 3145732
  278.9 76.7 %all-to-all-start.1 = ((bf16[64,8,256]{2,1,0:T(8,128)(2,1)}), bf16[64,8,256]{2,1,0:T(8,128)(2,1)S(1)}, u32[]{:S(2)}, u32[]{:S(2)}) async-start(bf16[64,8,256]{2,1,0:T(8,128)(2,1)} %fusion.8), calls=%async_computation.2 | async-start | bytes 524288 | tf_op jit(solution)/shard_map/all_to_all | solution.py:55
  355.7 70.6 %all-to-all-start.3 = ((bf16[64,8,256]{2,1,0:T(8,128)(2,1)}), bf16[64,8,256]{2,1,0:T(8,128)(2,1)S(1)}, u32[]{:S(2)}, u32[]{:S(2)}) async-start(bf16[64,8,256]{2,1,0:T(8,128)(2,1)} %fusion.7), calls=%async_computation.5 | async-start | bytes 524288 | tf_op jit(solution)/shard_map/all_to_all | solution.py:83
Sparse Core Ops, SparseCore 0:
  42.4 74.4 reduce-scatter.4
  120.3 80.7 reduce-scatter.2
  204.4 71.9 all-gather.2
  278.9 73.6 all-gather.4
where the time goes:
time: 434 us
  waiting for transfers between devices  272 us (63%)
  blocking collectives  101 us (23%)
  starting transfers between devices  21.1 us (5%)
  matrix products  16.3 us (4%)
  between operations  13.9 us (3%)
  other arithmetic  6.66 us (2%)
    reduce_scatter x1, waiting for transfers between devices, shards(): lax.psum_scatter(partial_value, 'dp', scatter_dimension=2, tiled=True)  84.2 us
    all_gather x1, waiting for transfers between devices, shards(): hidden_full = lax.all_gather(hidden_part, 'dp', axis=1, tiled=True)  72.1 us
    all_gather x1, waiting for transfers between devices, shards(): pair_full = lax.all_gather(pair_grad, 'dp', axis=2, tiled=True)  61.8 us
    psum x1, blocking collectives, shards(): gate_grad = lax.psum(jnp.sum(route_out * incoming, axis=2), 'dp')  54.9 us
    reduce_scatter x1, waiting for transfers between devices, shards(): lax.psum_scatter(hidden_partial, 'dp', scatter_dimension=1, tiled=True)  53.4 us
    all_to_all x1, blocking collectives, shards(): lax.all_to_all(grad_out, 'expert', split_axis=0, concat_axis=0, tiled=True)  28.2 us
    all_to_all x1, blocking collectives, shards(): lax.all_to_all(outgoing, 'expert', split_axis=0, concat_axis=0, tiled=True)  17.8 us
    all_to_all x1, starting transfers between devices, shards(): lax.all_to_all(expert_out.reshape(experts, capacity, slice_width), 'exper...  10.5 us
  transfers between devices with their start and end apart: 6, of which 4 were waited for; matrix products, arithmetic and copies ran while one was open for 4% of the time, Pallas kernels for 0%

commit v1 on v0

v1 whole, which is shorter than its diff:
```python
import jax
import jax.numpy as jnp
from jax import lax
from jax.sharding import PartitionSpec as P

F32 = jnp.float32
BF16 = jnp.bfloat16


def shards(tokens, routes, gates, counts, w_gate_up, w_down, cotangent):
    experts = lax.axis_size("expert")
    rows, width = tokens.shape
    top = routes.shape[1]
    cap = min(rows, 2 * rows * top // experts)
    slots = experts * cap
    ff = w_down.shape[2]
    pair_weight = w_gate_up[0]
    down_weight = w_down[0]

    slot_id = jnp.arange(slots, dtype=jnp.int32)
    slot_expert = slot_id // cap
    slot_pos = slot_id % cap
    named = routes[:, :, None] == slot_expert[None, None, :]
    member = jnp.any(named, axis=1).astype(BF16)
    earlier = jnp.tril(jnp.ones((rows, rows), BF16), -1)
    before = jnp.dot(earlier, member, preferred_element_type=F32)
    place = jnp.where(before == slot_pos[None, :].astype(F32), member, jnp.zeros((), BF16))
    gate_of = jnp.sum(jnp.where(named, gates[:, :, None], 0.0), axis=1) * place.astype(F32)
    gate_slot = jnp.sum(gate_of, axis=0)

    both = jnp.concatenate([tokens, cotangent], axis=1)
    picked = lax.dot_general(place, both, (((0,), (0,)), ((), ())), preferred_element_type=F32)
    scale = jnp.where(jnp.arange(2 * width)[None, :] < width, 1.0, gate_slot[:, None])
    outgoing = (picked * scale).astype(BF16).reshape(experts, cap, 2 * width)
    arrived = lax.all_to_all(outgoing, "expert", split_axis=0, concat_axis=0, tiled=True)
    arrived = arrived.reshape(slots, 2 * width)
    rows_in = arrived[:, :width]
    grad_rows = arrived[:, width:]

    pair_part = lax.dot_general(
        pair_weight, rows_in, (((0,), (1,)), ((), ())), preferred_element_type=F32
    )
    hidden_grad_part = lax.dot_general(
        down_weight, grad_rows, (((0,), (1,)), ((), ())), preferred_element_type=F32
    )
    ranks = lax.axis_size("dp")
    part_ff = ff // ranks
    part = jnp.concatenate([pair_part, hidden_grad_part[None]], axis=0)
    part = part.reshape(3, ranks, part_ff, slots).transpose(1, 0, 2, 3)
    part = part.reshape(3 * ff, slots)
    sums = lax.psum_scatter(part, "dp", scatter_dimension=0, tiled=True)
    gate_part = sums[:part_ff]
    up_part = sums[part_ff : 2 * part_ff]
    hidden_grad = sums[2 * part_ff :]
    sig_gate = jax.nn.sigmoid(gate_part)
    silu_gate = gate_part * sig_gate
    hidden_value = silu_gate * up_part
    slope_term = sig_gate * (1.0 + gate_part * (1.0 - sig_gate))
    gate_dot = jnp.sum(hidden_value * hidden_grad, axis=0)
    dot_hi = gate_dot.astype(BF16)
    dot_lo = (gate_dot - dot_hi.astype(F32)).astype(BF16)
    extra = jnp.concatenate(
        [dot_hi[None], dot_lo[None], jnp.zeros((14, slots), BF16)], axis=0
    )
    payload = jnp.concatenate(
        [
            hidden_value.astype(BF16),
            (hidden_grad * up_part * slope_term).astype(BF16),
            (hidden_grad * silu_gate).astype(BF16),
            extra,
        ],
        axis=0,
    )
    full = lax.all_gather(payload, "dp", axis=0, tiled=False)
    hidden_full = full[:, :part_ff].reshape(ff, slots)
    gate_grad_full = full[:, part_ff : 2 * part_ff].reshape(ff, slots)
    up_grad_full = full[:, 2 * part_ff : 3 * part_ff].reshape(ff, slots)
    pair_full = jnp.stack([gate_grad_full, up_grad_full], axis=0)
    dots = full[:, 3 * part_ff : 3 * part_ff + 2]
    dot_slot = jnp.sum(dots.astype(F32), axis=(0, 1))

    expert_out = lax.dot_general(
        hidden_full, down_weight, (((0,), (1,)), ((), ())), preferred_element_type=F32
    ).astype(BF16)
    row_grad = lax.dot_general(
        pair_full, pair_weight, (((0, 1), (1, 2)), ((), ())), preferred_element_type=F32
    ).astype(BF16)
    slot_hi = dot_slot.astype(BF16)
    slot_lo = (dot_slot - slot_hi.astype(F32)).astype(BF16)
    tail = jnp.concatenate(
        [slot_hi[:, None], slot_lo[:, None], jnp.zeros((slots, 126), BF16)], axis=1
    )
    back = jnp.concatenate([expert_out, row_grad, tail], axis=1)
    returned = lax.all_to_all(
        back.reshape(experts, cap, 2 * width + 128),
        "expert",
        split_axis=0,
        concat_axis=0,
        tiled=True,
    ).reshape(slots, 2 * width + 128)

    shares = counts.astype(F32) / jnp.sum(counts.astype(F32))
    slot_share = jnp.repeat(shares, cap)
    weighted_pair = (slot_share[None, None, :] * pair_full.astype(F32)).astype(BF16)
    weighted_hidden = (slot_share[None, :] * hidden_full.astype(F32)).astype(BF16)
    pair_update = lax.dot_general(
        rows_in, weighted_pair, (((0,), (2,)), ((), ())), preferred_element_type=F32
    ).astype(BF16)
    down_update = lax.dot_general(
        grad_rows, weighted_hidden, (((0,), (1,)), ((), ())), preferred_element_type=F32
    ).astype(BF16)
    weight_grads = jnp.concatenate([pair_update, down_update[:, None, :]], axis=1)

    gate_hi = gate_of.astype(BF16)
    gate_lo = (gate_of - gate_hi.astype(F32)).astype(BF16)
    combine = jnp.concatenate([gate_hi, gate_lo], axis=0)
    mixed_parts = jnp.dot(combine, returned[:, :width], preferred_element_type=F32)
    mixed = (mixed_parts[:rows] + mixed_parts[rows:]).astype(BF16)
    token_grad = jnp.dot(
        place, returned[:, width : 2 * width], preferred_element_type=F32
    ).astype(BF16)
    dot_back = jnp.sum(returned[:, 2 * width : 2 * width + 2].astype(F32), axis=1)
    at_slot = place.astype(F32) * dot_back[None, :]
    gate_grad = jnp.sum(jnp.where(named, at_slot[:, None, :], 0.0), axis=2) / gates
    return (mixed, gate_grad, token_grad, weight_grads[None])


def solution(mesh):
    return jax.shard_map(
        shards,
        mesh=mesh,
        in_specs=(
            P("expert", "dp"),
            P("expert", None),
            P("expert", None),
            P(),
            P("expert", "dp", None, None),
            P("expert", "dp", None),
            P("expert", "dp"),
        ),
        out_specs=(
            P("expert", "dp"),
            P("expert", None),
            P("expert", "dp"),
            P("expert", "dp", None, None),
        ),
        check_vma=False,
    )
```

time: 434 us -> 292 us (0.67)
  waiting for transfers between devices: 272 us -> 181 us
  blocking collectives: 101 us -> 33.4 us
  local copies, waits for them, and re-layouts: 2.98 us -> 26.1 us
  starting transfers between devices: 21.1 us -> 10.5 us
    all_gather x2 -> x1, waiting for transfers between devices: 134 us -> 78.2 us  [shards(): full = lax.all_gather(payload, 'dp', axis=0, tiled=False)]
    psum x1 -> x0, blocking collectives: 54.9 us -> none  [shards(): gate_grad = lax.psum(jnp.sum(route_out * incoming, axis=2), 'dp')]
    reduce_scatter x2 -> x1, waiting for transfers between devices: 138 us -> 90.1 us  [shards(): sums = lax.psum_scatter(part, 'dp', scatter_dimension=0, tiled=True)]
    all_to_all x1 -> x0, blocking collectives: 28.2 us -> none  [shards(): lax.all_to_all(grad_out, 'expert', split_axis=0, concat_axis=0, tiled=True)]
    all_to_all x1, blocking collectives: 17.8 us -> 33.4 us  [shards(): lax.all_to_all(outgoing, 'expert', split_axis=0, concat_axis=0, tiled=True)]
    all_to_all x2 -> x1, waiting for transfers between devices: 0.01 us -> 12.8 us  [shards(): lax.all_to_all(back.reshape(experts, cap, 2 * width + 128), 'expert', spl...]
    all_to_all x2 -> x1, starting transfers between devices: 20.9 us -> 10.5 us  [shards(): lax.all_to_all(back.reshape(experts, cap, 2 * width + 128), 'expert', spl...]
    dot_general x0 -> x2, local copies, waits for them, and re-layouts: none -> 7.27 us  [the longest x1 5.41 us: shards(): lax.dot_general(pair_weight, rows_in, (((0,), (1,)), ((), ())), preferred...]
  transfers between devices with their start and end apart: 6 -> 3, of which waited for: 4 -> 3; matrix products, arithmetic and copies ran while one was open for 4% -> 2% of each run, Pallas kernels for 0% -> 0%
where the time goes in v1:
time: 292 us; the launch traced here: 289 us
  waiting for transfers between devices  181 us (62%)
  blocking collectives  33.4 us (11%)
  local copies, waits for them, and re-layouts  26.1 us (9%)
  matrix products  14.4 us (5%)
  between operations  14.2 us (5%)
  starting transfers between devices  10.5 us (4%)
  other arithmetic  9.57 us (3%)
    reduce_scatter x1, waiting for transfers between devices, shards(): sums = lax.psum_scatter(part, 'dp', scatter_dimension=0, tiled=True)  90.1 us
    all_gather x1, waiting for transfers between devices, shards(): full = lax.all_gather(payload, 'dp', axis=0, tiled=False)  78.2 us
    all_to_all x1, blocking collectives, shards(): lax.all_to_all(outgoing, 'expert', split_axis=0, concat_axis=0, tiled=True)  33.4 us
    all_to_all x1, waiting for transfers between devices, shards(): lax.all_to_all(back.reshape(experts, cap, 2 * width + 128), 'expert', spl...  12.8 us
    all_to_all x1, starting transfers between devices, shards(): lax.all_to_all(back.reshape(experts, cap, 2 * width + 128), 'expert', spl...  10.5 us
  transfers between devices with their start and end apart: 3, of which 3 were waited for; matrix products, arithmetic and copies ran while one was open for 2% of the time, Pallas kernels for 0%

profile of v1, /device:TPU:6, one launch (start us, length us, event | category | flops | bytes accessed | tf_op | source)
XLA Modules:
  0.0 289.3 jit_solution(62580251526935930)
XLA Ops:
  7.3 0.8 copy.45
  8.1 0.8 copy.46
  9.5 1.1 fusion.6
  10.6 33.4 %all_to_all.10 = bf16[64,8,512]{2,1,0:T(8,128)(2,1)S(1)} all-to-all(bf16[64,8,512]{2,1,0:T(8,128)(2,1)S(1)} %fusion.6), channel_id=1, replica_groups=mesh['dp'=16,'expert'=64] {'expert'}, dimensions={0} | all-to-all | bytes 1048576 | tf_op jit(solution)/shard_map/all_to_all | solution.py:35
  44.0 0.8 copy-done.1
  44.9 2.8 convolution_bitcast_fusion
  47.6 5.4 %copy.48 = f32[2,1024,512]{2,1,0:T(8,128)} copy(f32[2,1024,512]{1,2,0:T(8,128)} %convolution_bitcast_fusion) | data formatting | bytes 8388608 | tf_op jit(solution)/shard_map/dot_general | solution.py:40
  53.0 1.6 convolution_bitcast_fusion.1
  54.6 1.9 copy.49
  56.5 3.5 %maximum_bitcast_fusion = f32[16,3,64,512]{3,2,0,1:T(8,128)S(1)} fusion(f32[1,16,64,512]{3,2,1,0:T(8,128)} %bitcast.51, f32[2,16,64,512]{3,2,1,0:T(8,128)} %bitcast.50), kind=kLoop, calls=%fused_computation | loop fusion | flops 1572864 | bytes 12582912 | tf_op jit(solution)/shard_map/transpose | solution.py:49
  60.0 3.4 %copy.50 = f32[16,3,64,512]{3,2,1,0:T(8,128)} copy(f32[16,3,64,512]{3,2,0,1:T(8,128)S(1)} %maximum_bitcast_fusion) | data formatting | bytes 12582912 | tf_op jit(solution)/shard_map/transpose | solution.py:49
  63.4 90.1 %reduce-scatter.2.cloned.1.call-done = f32[192,512]{1,0:T(8,128)} async-done(((f32[3072,512]{1,0:T(8,128)}), f32[192,512]{1,0:T(8,128)}) %reduce-scatter.2.cloned.1.call-update) | async-done | bytes 393232 | tf_op jit(solution)/shard_map/reduce_scatter | solution.py:51
  153.5 1.1 multiply_reduce_fusion
  154.7 3.8 %concatenate.33 = bf16[208,512]{1,0:T(8,128)(2,1)} concatenate(bf16[64,512]{1,0:T(8,128)(2,1)S(1)} %get-tuple-element.20, bf16[64,512]{1,0:T(8,128)(2,1)S(1)} %get-tuple-element.18, bf16[64,512]{1,0:T(8,128)(2,1)S(1)} %get-tuple-element.19, bf16[1,512]{1,0:T(2,128)(2,1)S(1)} %convert_element_type.158, bf16[1,512]{1,0:T(2,128)(2,1)S(1)} %subtract_convert_fusion.2, ...), dimensions={0} | concatenate | bytes 425984 | tf_op jit(solution)/shard_map/concatenate | solution.py:65
  158.6 78.2 %all-gather.3.cloned.1.call-done = bf16[3328,512]{1,0:T(8,128)(2,1)} async-done(((bf16[208,512]{1,0:T(8,128)(2,1)}), bf16[3328,512]{1,0:T(8,128)(2,1)}) %all-gather.3.cloned.1.call-update) | async-done | bytes 3407888 | tf_op jit(solution)/shard_map/all_gather | solution.py:74
  236.7 3.1 %fusion.54 = (bf16[16,64,512]{2,1,0:T(8,128)(2,1)S(1)}, bf16[16,64,512]{2,1,0:T(8,128)(2,1)S(1)}, bf16[16,64,512]{2,1,0:T(8,128)(2,1)}) fusion(bf16[16,208,512]{2,1,0:T(8,128)(2,1)} %bitcast.54), kind=kLoop, calls=%fused_computation.91 | loop fusion | bytes 6291456 | tf_op jit(solution)/shard_map/slice | solution.py:76
  239.9 1.0 convert_reduce_fusion.1
  240.8 1.3 copy.51
  242.1 1.3 copy.52
  243.5 2.7 fusion.10
  246.7 1.5 fusion.9
  248.2 2.0 concatenate.36
  250.2 10.5 %all-to-all-start.1 = ((bf16[64,8,640]{2,1,0:T(8,128)(2,1)}), bf16[64,8,640]{2,1,0:T(8,128)(2,1)S(1)}, u32[]{:S(2)}, u32[]{:S(2)}) async-start(bf16[64,8,640]{2,1,0:T(8,128)(2,1)} %concatenate.36), calls=%async_computation.2 | async-start | bytes 1310720 | tf_op jit(solution)/shard_map/all_to_all | solution.py:94
  260.7 0.6 convert_reduce_fusion.2
  261.3 0.6 convert_divide_fusion
  262.1 1.7 fusion.5
  263.8 2.0 fusion.2
  265.9 1.3 maximum_bitcast_fusion.1
  267.1 12.8 %all-to-all-done.1 = bf16[64,8,640]{2,1,0:T(8,128)(2,1)S(1)} async-done(((bf16[64,8,640]{2,1,0:T(8,128)(2,1)}), bf16[64,8,640]{2,1,0:T(8,128)(2,1)S(1)}, u32[]{:S(2)}, u32[]{:S(2)}) %all-to-all-start.1) | async-done | bytes 655392 | tf_op jit(solution)/shard_map/all_to_all | solution.py:94
  279.9 0.8 convolution_convert_fusion.2
  281.0 0.7 copy.61
  281.8 0.6 fusion.29
  (38 shorter events, 2.0 us)
Async XLA Ops:
  7.2 36.9 %copy-start = (bf16[1,256,2,1024]{3,2,1,0:T(2,128)(2,1)S(1)}, bf16[1,256,2,1024]{3,2,1,0:T(2,128)(2,1)}, u32[]{:S(2)}) copy-start(bf16[1,256,2,1024]{3,2,1,0:T(2,128)(2,1)} %param.11) | copy-start | bytes 3145732
  7.2 146.4 %reduce-scatter.2.cloned.1.call-start = ((), (), s32[]{:S(2)}) async-start(), calls=%async_computation.3 | async-start | bytes 6684672 | tf_op jit(solution)/shard_map/reduce_scatter | solution.py:51
  44.0 0.8 copy-start.1
  63.4 173.4 %all-gather.3.cloned.1.call-start = ((), (), s32[]{:S(2)}) async-start(), calls=%async_computation.4 | async-start | bytes 3620864 | tf_op jit(solution)/shard_map/all_gather | solution.py:74
  242.1 4.5 %copy-start.3 = (bf16[1,1024,512]{1,2,0:T(8,128)(2,1)S(1)}, bf16[1,1024,512]{1,2,0:T(8,128)(2,1)}, u32[]{:S(2)}) copy-start(bf16[1,1024,512]{1,2,0:T(8,128)(2,1)} %copy.51) | copy-start | bytes 3145732
  243.5 3.2 %copy-start.4 = (bf16[1,1024,512]{1,2,0:T(8,128)(2,1)S(1)}, bf16[1,1024,512]{1,2,0:T(8,128)(2,1)}, u32[]{:S(2)}) copy-start(bf16[1,1024,512]{1,2,0:T(8,128)(2,1)} %copy.52) | copy-start | bytes 3145732
  248.1 12.5 %copy-start.5 = (s32[64]{0:T(128)S(1)}, s32[64]{0:T(128)}, u32[]{:S(2)}) copy-start(s32[64]{0:T(128)} %param.10) | copy-start | bytes 772
  248.1 13.9 %copy-start.2 = (bf16[64,8,512]{2,1,0:T(8,128)(2,1)S(1)}, bf16[64,8,512]{2,1,0:T(8,128)(2,1)}, u32[]{:S(2)}) copy-start(bf16[64,8,512]{2,1,0:T(8,128)(2,1)} %copy-done.1) | copy-start | bytes 1572868
  250.2 29.7 %all-to-all-start.1 = ((bf16[64,8,640]{2,1,0:T(8,128)(2,1)}), bf16[64,8,640]{2,1,0:T(8,128)(2,1)S(1)}, u32[]{:S(2)}, u32[]{:S(2)}) async-start(bf16[64,8,640]{2,1,0:T(8,128)(2,1)} %concatenate.36), calls=%async_computation.2 | async-start | bytes 1310720 | tf_op jit(solution)/shard_map/all_to_all | solution.py:94
Sparse Core Ops, SparseCore 0:
  63.5 89.9 reduce-scatter.1
  158.7 78.0 all-gather.2

commit v2 on v1

v2 whole, which is shorter than its diff:
```python
import jax
import jax.numpy as jnp
from jax import lax
from jax.sharding import PartitionSpec as P

F32 = jnp.float32
BF16 = jnp.bfloat16


def shards(tokens, routes, gates, counts, w_gate_up, w_down, cotangent):
    experts = lax.axis_size("expert")
    rows, width = tokens.shape
    top = routes.shape[1]
    cap = min(rows, 2 * rows * top // experts)
    slots = experts * cap
    ff = w_down.shape[2]
    pair_weight = w_gate_up[0]
    down_weight = w_down[0]

    slot_id = jnp.arange(slots, dtype=jnp.int32)
    slot_expert = slot_id // cap
    slot_pos = slot_id % cap
    named = routes[:, :, None] == slot_expert[None, None, :]
    member = jnp.any(named, axis=1).astype(BF16)
    earlier = jnp.tril(jnp.ones((rows, rows), BF16), -1)
    before = jnp.dot(earlier, member, preferred_element_type=F32)
    place = jnp.where(before == slot_pos[None, :].astype(F32), member, jnp.zeros((), BF16))
    gate_of = jnp.sum(jnp.where(named, gates[:, :, None], 0.0), axis=1) * place.astype(F32)
    gate_slot = jnp.sum(gate_of, axis=0)

    both = jnp.concatenate([tokens, cotangent], axis=1)
    picked = lax.dot_general(place, both, (((0,), (0,)), ((), ())), preferred_element_type=F32)
    scale = jnp.where(jnp.arange(2 * width)[None, :] < width, 1.0, gate_slot[:, None])
    outgoing = (picked * scale).astype(BF16).reshape(experts, cap, 2 * width)
    arrived = lax.all_to_all(outgoing, "expert", split_axis=0, concat_axis=0, tiled=True)
    arrived = arrived.reshape(slots, 2 * width)
    rows_in = arrived[:, :width]
    grad_rows = arrived[:, width:]

    pair_part = lax.dot_general(
        rows_in, pair_weight, (((1,), (0,)), ((), ())), preferred_element_type=F32
    )
    hidden_grad_part = jnp.dot(grad_rows, down_weight, preferred_element_type=F32)
    part = jnp.concatenate([pair_part, hidden_grad_part[:, None, :]], axis=1)
    sums = lax.psum_scatter(part, "dp", scatter_dimension=0, tiled=True)
    gate_part, up_part, hidden_grad = sums[:, 0], sums[:, 1], sums[:, 2]
    sig_gate = jax.nn.sigmoid(gate_part)
    silu_gate = gate_part * sig_gate
    hidden_value = silu_gate * up_part
    slope_term = sig_gate * (1.0 + gate_part * (1.0 - sig_gate))
    gate_dot = jnp.sum(hidden_value * hidden_grad, axis=1)
    hidden = hidden_value.astype(BF16)
    gate_grad_part = (hidden_grad * up_part * slope_term).astype(BF16)
    up_grad_part = (hidden_grad * silu_gate).astype(BF16)
    later_weight, _ = lax.optimization_barrier((pair_weight, part))
    flat_weight = later_weight.reshape(width, 2 * ff)

    ranks = lax.axis_size("dp")
    half = ranks // 2
    same_parity = [[2 * i + q for i in range(half)] for q in range(2)]
    to_right = [(i, (i + 1) % ranks) for i in range(ranks)]
    to_left = [(i, (i - 1) % ranks) for i in range(ranks)]
    is_even = lax.axis_index("dp") % 2 == 0

    def gather(value):
        own = lax.all_gather(value, "dp", axis=0, tiled=False, axis_index_groups=same_parity)
        first = lax.ppermute(own[: half // 2], "dp", to_right)
        second = lax.ppermute(own[half // 2 :], "dp", to_left)
        other = jnp.concatenate([first, second], axis=0)
        even = jnp.where(is_even, own, other)
        odd = jnp.where(is_even, other, own)
        return jnp.stack([even, odd], axis=1).reshape(slots, value.shape[1])

    dot_hi = gate_dot.astype(BF16)
    dot_lo = (gate_dot - dot_hi.astype(F32)).astype(BF16)
    lane = jnp.arange(128)[None, :]
    dots = jnp.where(lane == 0, dot_hi[:, None], jnp.where(lane == 1, dot_lo[:, None], jnp.zeros((), BF16)))
    gathered = gather(jnp.concatenate([hidden, dots], axis=1))
    hidden_full = gathered[:, :ff]
    gate_grad_full = gather(gate_grad_part)
    up_grad_full = gather(up_grad_part)

    expert_out = lax.dot_general(
        hidden_full, down_weight, (((1,), (1,)), ((), ())), preferred_element_type=F32
    ).astype(BF16)
    row_grad = (
        lax.dot_general(
            gate_grad_full, flat_weight[:, :ff], (((1,), (1,)), ((), ())), preferred_element_type=F32
        )
        + lax.dot_general(
            up_grad_full, flat_weight[:, ff:], (((1,), (1,)), ((), ())), preferred_element_type=F32
        )
    ).astype(BF16)

    def send_back(value):
        sent = value.reshape(experts, cap, value.shape[1])
        came = lax.all_to_all(sent, "expert", split_axis=0, concat_axis=0, tiled=True)
        return came.reshape(slots, value.shape[1])

    first_back = send_back(jnp.concatenate([expert_out, gathered[:, ff:]], axis=1))
    grad_back = send_back(row_grad)
    out_back = first_back[:, :width]
    dot_back = jnp.sum(first_back[:, width:].astype(F32), axis=1)
    at_slot = place.astype(F32) * dot_back[None, :]
    gate_grad = jnp.sum(jnp.where(named, at_slot[:, None, :], 0.0), axis=2) / gates

    shares = counts.astype(F32) / jnp.sum(counts.astype(F32))
    slot_share = jnp.repeat(shares, cap)[:, None]
    weighted_gate = (slot_share * gate_grad_full.astype(F32)).astype(BF16)
    weighted_up = (slot_share * up_grad_full.astype(F32)).astype(BF16)
    weighted_hidden = (slot_share * hidden_full.astype(F32)).astype(BF16)
    gate_update = lax.dot_general(
        rows_in, weighted_gate, (((0,), (0,)), ((), ())), preferred_element_type=F32
    ).astype(BF16)
    up_update = lax.dot_general(
        rows_in, weighted_up, (((0,), (0,)), ((), ())), preferred_element_type=F32
    ).astype(BF16)
    down_update = lax.dot_general(
        grad_rows, weighted_hidden, (((0,), (0,)), ((), ())), preferred_element_type=F32
    ).astype(BF16)
    weight_grads = jnp.stack([gate_update, up_update, down_update], axis=1)

    gate_hi = gate_of.astype(BF16)
    gate_lo = (gate_of - gate_hi.astype(F32)).astype(BF16)
    combine = jnp.concatenate([gate_hi, gate_lo], axis=0)
    mixed_parts = jnp.dot(combine, out_back, preferred_element_type=F32)
    mixed = (mixed_parts[:rows] + mixed_parts[rows:]).astype(BF16)
    token_grad = jnp.dot(place, grad_back, preferred_element_type=F32).astype(BF16)
    return (mixed, gate_grad, token_grad, weight_grads[None])


def solution(mesh):
    return jax.shard_map(
        shards,
        mesh=mesh,
        in_specs=(
            P("expert", "dp"),
            P("expert", None),
            P("expert", None),
            P(),
            P("expert", "dp", None, None),
            P("expert", "dp", None),
            P("expert", "dp"),
        ),
        out_specs=(
            P("expert", "dp"),
            P("expert", None),
            P("expert", "dp"),
            P("expert", "dp", None, None),
        ),
        check_vma=False,
    )
```

time: 292 us -> 312 us (1.068)
  blocking collectives: 33.4 us -> 126 us
  waiting for transfers between devices: 181 us -> 106 us
  starting transfers between devices: 10.5 us -> 37.9 us
  local copies, waits for them, and re-layouts: 26.1 us -> 6.55 us
  matrix products: 14.4 us -> 9.83 us
    all_gather x0 -> x3, blocking collectives: none -> 92.4 us  [gather(): lax.all_gather(value, 'dp', axis=0, tiled=False, axis_index_groups=same_p...]
    all_gather x1 -> x0, waiting for transfers between devices: 78.2 us -> none  [shards(): full = lax.all_gather(payload, 'dp', axis=0, tiled=False)]
    ppermute x0 -> x6, starting transfers between devices: none -> 21.1 us  [the longest x3 15.2 us: gather(): second = lax.ppermute(own[half // 2:], 'dp', to_left)]
    dot_general x2 -> x0, local copies, waits for them, and re-layouts: 7.27 us -> none  [the longest x1 5.41 us: shards(): lax.dot_general(pair_weight, rows_in, (((0,), (1,)), ((), ())), preferred...]
    all_to_all x1 -> x2, starting transfers between devices: 10.5 us -> 16.7 us  [send_back(): lax.all_to_all(sent, 'expert', split_axis=0, concat_axis=0, tiled=True)]
    all_to_all x1 -> x2, waiting for transfers between devices: 12.8 us -> 18.3 us  [send_back(): lax.all_to_all(sent, 'expert', split_axis=0, concat_axis=0, tiled=True)]
    dot_general x8 -> x10, matrix products: 13.1 us -> 7.96 us  [the longest x1 1.82 us: shards(): lax.dot_general(rows_in, weighted_gate, (((0,), (0,)), ((), ())), preferr...]
    concatenate x2 -> x4, local copies, waits for them, and re-layouts: 5.87 us -> 1.96 us  [the longest x3 1.03 us: gather(): other = jnp.concatenate([first, second], axis=0)]
  transfers between devices with their start and end apart: 3 -> 9, of which waited for: 3 -> 3; matrix products, arithmetic and copies ran while one was open for 2% -> 4% of each run, Pallas kernels for 0% -> 0%
where the time goes in v2:
time: 312 us; the launch traced here: 310 us
  blocking collectives  126 us (40%)
  waiting for transfers between devices  106 us (34%)
  starting transfers between devices  37.9 us (12%)
  between operations  14.5 us (5%)
  matrix products  9.83 us (3%)
  other arithmetic  9.23 us (3%)
  local copies, waits for them, and re-layouts  6.55 us (2%)
    all_gather x3, blocking collectives, gather(): lax.all_gather(value, 'dp', axis=0, tiled=False, axis_index_groups=same_p...  92.4 us
    reduce_scatter x1, waiting for transfers between devices, shards(): sums = lax.psum_scatter(part, 'dp', scatter_dimension=0, tiled=True)  87.8 us
    all_to_all x1, blocking collectives, shards(): lax.all_to_all(outgoing, 'expert', split_axis=0, concat_axis=0, tiled=True)  33.4 us
    all_to_all x2, waiting for transfers between devices, send_back(): lax.all_to_all(sent, 'expert', split_axis=0, concat_axis=0, tiled=True)  18.3 us
    all_to_all x2, starting transfers between devices, send_back(): lax.all_to_all(sent, 'expert', split_axis=0, concat_axis=0, tiled=True)  16.7 us
    ppermute x3, starting transfers between devices, gather(): second = lax.ppermute(own[half // 2:], 'dp', to_left)  15.2 us
  transfers between devices with their start and end apart: 9, of which 3 were waited for; matrix products, arithmetic and copies ran while one was open for 4% of the time, Pallas kernels for 0%

profile of v2, /device:TPU:6, one launch (start us, length us, event | category | flops | bytes accessed | tf_op | source)
XLA Modules:
  0.0 310.0 jit_solution(12468882695437676936)
XLA Ops:
  7.3 0.9 copy.31
  8.2 0.8 copy.32
  9.4 0.8 fusion.52
  10.2 1.1 fusion.4
  11.3 33.4 %all_to_all.15 = bf16[64,8,512]{2,1,0:T(8,128)(2,1)S(1)} all-to-all(bf16[64,8,512]{2,1,0:T(8,128)(2,1)S(1)} %fusion.4), channel_id=1, replica_groups=mesh['dp'=16,'expert'=64] {'expert'}, dimensions={0} | all-to-all | bytes 1048576 | tf_op jit(solution)/shard_map/all_to_all | solution.py:35
  44.7 0.8 fusion.8
  45.9 3.2 %pad_maximum_fusion = f32[512,3,1024]{2,0,1:T(8,128)} fusion(f32[512,1,1024]{2,0,1:T(8,128)S(1)} %convolution_bitcast_fusion, f32[512,2,1024]{2,0,1:T(8,128)S(1)} %fusion.8), kind=kLoop, calls=%fused_computation | loop fusion | flops 1572864 | bytes 12582912 | tf_op jit(solution)/shard_map/concatenate | solution.py:44
  50.4 0.6 convert_divide_fusion
  51.5 87.8 %reduce-scatter.2.cloned.1.call-done = f32[32,3,1024]{2,0,1:T(8,128)} async-done(((f32[512,3,1024]{2,0,1:T(8,128)}), f32[32,3,1024]{2,0,1:T(8,128)}) %reduce-scatter.2.cloned.1.call-update) | async-done | bytes 393232 | tf_op jit(solution)/shard_map/reduce_scatter | solution.py:45
  139.3 1.2 fusion.39
  140.4 31.5 %all_gather.17 = bf16[8,32,1024]{2,1,0:T(8,128)(2,1)S(1)} all-gather(bf16[1,32,1024]{2,1,0:T(8,128)(2,1)S(1)} %get-tuple-element.22), channel_id=1, replica_groups={{0,128,256,384,512,640,768,896},{64,192,320,448,576,704,832,960},{1,129..., dimensions={0}, use_global_device_ids=true | all-gather | bytes 589824 | tf_op jit(solution)/shard_map/all_gather | solution.py:66
  172.0 2.1 collective-permute-start.4
  174.1 5.0 %collective-permute-start.5 = (bf16[4,32,1024]{2,1,0:T(8,128)(2,1)S(1)}, bf16[4,32,1024]{2,1,0:T(8,128)(2,1)S(1)}, u32[]{:S(2)}, u32[]{:S(2)}) collective-permute-start(bf16[4,32,1024]{2,1,0:T(8,128)(2,1)S(1)} %get-tuple-element.18), channel_id=1, source_target_pairs={{0,960},{64,0},{128,64},{192,128},{256,192},{320,256},{384,320},{4... | collective-permute-start | bytes 786440 | tf_op jit(solution)/shard_map/ppermute | solution.py:68
  179.0 30.6 %all_gather.16 = bf16[8,32,1024]{2,1,0:T(8,128)(2,1)S(1)} all-gather(bf16[1,32,1024]{2,1,0:T(8,128)(2,1)S(1)} %get-tuple-element.23), channel_id=1, replica_groups={{0,128,256,384,512,640,768,896},{64,192,320,448,576,704,832,960},{1,129..., dimensions={0}, use_global_device_ids=true | all-gather | bytes 589824 | tf_op jit(solution)/shard_map/all_gather | solution.py:66
  209.7 1.9 collective-permute-start.2
  211.6 5.1 %collective-permute-start.3 = (bf16[4,32,1024]{2,1,0:T(8,128)(2,1)S(1)}, bf16[4,32,1024]{2,1,0:T(8,128)(2,1)S(1)}, u32[]{:S(2)}, u32[]{:S(2)}) collective-permute-start(bf16[4,32,1024]{2,1,0:T(8,128)(2,1)S(1)} %get-tuple-element.20), channel_id=1, source_target_pairs={{0,960},{64,0},{128,64},{192,128},{256,192},{320,256},{384,320},{4... | collective-permute-start | bytes 786440 | tf_op jit(solution)/shard_map/ppermute | solution.py:68
  217.0 30.3 %all-gather = bf16[256,1152]{1,0:T(8,128)(2,1)S(1)} all-gather(bf16[32,1152]{1,0:T(8,128)(2,1)S(1)} %pad_maximum_fusion.5), channel_id=2, replica_groups={{0,128,256,384,512,640,768,896},{64,192,320,448,576,704,832,960},{1,129..., dimensions={0}, use_global_device_ids=true | all-gather | bytes 663552 | tf_op jit(solution)/shard_map/all_gather | solution.py:66
  247.3 0.9 fusion.71
  248.2 1.9 collective-permute-start
  250.1 5.1 %collective-permute-start.1 = (bf16[4,32,1152]{2,1,0:T(8,128)(2,1)}, bf16[4,32,1152]{2,1,0:T(8,128)(2,1)}, u32[]{:S(2)}, u32[]{:S(2)}) collective-permute-start(bf16[4,32,1152]{2,1,0:T(8,128)(2,1)} %bitcast.11), channel_id=1, source_target_pairs={{0,960},{64,0},{128,64},{192,128},{256,192},{320,256},{384,320},{4... | collective-permute-start | bytes 884744 | tf_op jit(solution)/shard_map/ppermute | solution.py:68
  256.4 1.2 fusion.6
  257.5 1.3 fusion.2
  258.9 10.3 %all-to-all-start.2 = ((bf16[64,8,256]{2,1,0:T(8,128)(2,1)}), bf16[64,8,256]{2,1,0:T(8,128)(2,1)S(1)}, u32[]{:S(2)}, u32[]{:S(2)}) async-start(bf16[64,8,256]{2,1,0:T(8,128)(2,1)} %fusion.6), calls=%async_computation.3 | async-start | bytes 524288 | tf_op jit(solution)/shard_map/all_to_all | solution.py:97
  269.2 1.0 constant_dynamic-update-slice_fusion
  271.1 0.9 copy.36
  272.0 8.7 %all-to-all-done.2 = bf16[64,8,256]{2,1,0:T(8,128)(2,1)S(1)} async-done(((bf16[64,8,256]{2,1,0:T(8,128)(2,1)}), bf16[64,8,256]{2,1,0:T(8,128)(2,1)S(1)}, u32[]{:S(2)}, u32[]{:S(2)}) %all-to-all-start.2) | async-done | bytes 262176 | tf_op jit(solution)/shard_map/all_to_all | solution.py:97
  280.7 6.5 %all-to-all-start.1 = ((bf16[64,8,384]{2,1,0:T(8,128)(2,1)}), bf16[64,8,384]{2,1,0:T(8,128)(2,1)S(1)}, u32[]{:S(2)}, u32[]{:S(2)}) async-start(bf16[64,8,384]{2,1,0:T(8,128)(2,1)} %bitcast.16), calls=%async_computation.2 | async-start | bytes 786432 | tf_op jit(solution)/shard_map/all_to_all | solution.py:97
  287.2 1.8 fusion.1
  289.6 1.3 maximum_bitcast_fusion
  290.9 0.8 convolution_convert_fusion.4
  291.7 9.6 %all-to-all-done.1 = bf16[64,8,384]{2,1,0:T(8,128)(2,1)S(1)} async-done(((bf16[64,8,384]{2,1,0:T(8,128)(2,1)}), bf16[64,8,384]{2,1,0:T(8,128)(2,1)S(1)}, u32[]{:S(2)}, u32[]{:S(2)}) %all-to-all-start.1) | async-done | bytes 393248 | tf_op jit(solution)/shard_map/all_to_all | solution.py:97
  301.7 0.7 copy.40
  (64 shorter events, 6.5 us)
Async XLA Ops:
  7.2 38.3 %copy-start = (bf16[1,256,1024]{2,1,0:T(8,128)(2,1)S(1)}, bf16[1,256,1024]{2,1,0:T(8,128)(2,1)}, u32[]{:S(2)}) copy-start(bf16[1,256,1024]{2,1,0:T(8,128)(2,1)} %param.12) | copy-start | bytes 1572868
  7.2 37.5 %copy-start.1 = (bf16[1,256,2,1024]{3,2,1,0:T(2,128)(2,1)S(1)}, bf16[1,256,2,1024]{3,2,1,0:T(2,128)(2,1)}, u32[]{:S(2)}) copy-start(bf16[1,256,2,1024]{3,2,1,0:T(2,128)(2,1)} %param.11) | copy-start | bytes 3145732
  7.2 132.1 %reduce-scatter.2.cloned.1.call-start = ((), (), s32[]{:S(2)}) async-start(), calls=%async_computation.4 | async-start | bytes 6684672 | tf_op jit(solution)/shard_map/reduce_scatter | solution.py:45
  49.1 0.7 copy-start.6
  139.3 77.5 %copy-start.2 = (f32[32,3,1024]{2,0,1:T(8,128)S(1)}, f32[32,3,1024]{2,0,1:T(8,128)}, u32[]{:S(2)}) copy-start(f32[32,3,1024]{2,0,1:T(8,128)} %reduce-scatter.2.cloned.1.call-done) | copy-start | bytes 1179652
  172.0 78.1 %collective-permute-start.4 = (bf16[4,32,1024]{2,1,0:T(8,128)(2,1)S(1)}, bf16[4,32,1024]{2,1,0:T(8,128)(2,1)S(1)}, u32[]{:S(2)}, u32[]{:S(2)}) collective-permute-start(bf16[4,32,1024]{2,1,0:T(8,128)(2,1)S(1)} %get-tuple-element.19), channel_id=1, source_target_pairs={{0,64},{64,128},{128,192},{192,256},{256,320},{320,384},{384,448},... | collective-permute-start | bytes 786440 | tf_op jit(solution)/shard_map/ppermute | solution.py:67
  174.1 81.2 %collective-permute-start.5 = (bf16[4,32,1024]{2,1,0:T(8,128)(2,1)S(1)}, bf16[4,32,1024]{2,1,0:T(8,128)(2,1)S(1)}, u32[]{:S(2)}, u32[]{:S(2)}) collective-permute-start(bf16[4,32,1024]{2,1,0:T(8,128)(2,1)S(1)} %get-tuple-element.18), channel_id=1, source_target_pairs={{0,960},{64,0},{128,64},{192,128},{256,192},{320,256},{384,320},{4... | collective-permute-start | bytes 786440 | tf_op jit(solution)/shard_map/ppermute | solution.py:68
  209.7 45.9 %collective-permute-start.2 = (bf16[4,32,1024]{2,1,0:T(8,128)(2,1)S(1)}, bf16[4,32,1024]{2,1,0:T(8,128)(2,1)S(1)}, u32[]{:S(2)}, u32[]{:S(2)}) collective-permute-start(bf16[4,32,1024]{2,1,0:T(8,128)(2,1)S(1)} %get-tuple-element.21), channel_id=1, source_target_pairs={{0,64},{64,128},{128,192},{192,256},{256,320},{320,384},{384,448},... | collective-permute-start | bytes 786440 | tf_op jit(solution)/shard_map/ppermute | solution.py:67
  211.6 44.0 %collective-permute-start.3 = (bf16[4,32,1024]{2,1,0:T(8,128)(2,1)S(1)}, bf16[4,32,1024]{2,1,0:T(8,128)(2,1)S(1)}, u32[]{:S(2)}, u32[]{:S(2)}) collective-permute-start(bf16[4,32,1024]{2,1,0:T(8,128)(2,1)S(1)} %get-tuple-element.20), channel_id=1, source_target_pairs={{0,960},{64,0},{128,64},{192,128},{256,192},{320,256},{384,320},{4... | collective-permute-start | bytes 786440 | tf_op jit(solution)/shard_map/ppermute | solution.py:68
  248.2 21.0 %collective-permute-start = (bf16[4,32,1152]{2,1,0:T(8,128)(2,1)}, bf16[4,32,1152]{2,1,0:T(8,128)(2,1)S(1)}, u32[]{:S(2)}, u32[]{:S(2)}) collective-permute-start(bf16[4,32,1152]{2,1,0:T(8,128)(2,1)} %bitcast.10), channel_id=1, source_target_pairs={{0,64},{64,128},{128,192},{192,256},{256,320},{320,384},{384,448},... | collective-permute-start | bytes 884744 | tf_op jit(solution)/shard_map/ppermute | solution.py:67
  250.1 19.1 %collective-permute-start.1 = (bf16[4,32,1152]{2,1,0:T(8,128)(2,1)}, bf16[4,32,1152]{2,1,0:T(8,128)(2,1)}, u32[]{:S(2)}, u32[]{:S(2)}) collective-permute-start(bf16[4,32,1152]{2,1,0:T(8,128)(2,1)} %bitcast.11), channel_id=1, source_target_pairs={{0,960},{64,0},{128,64},{192,128},{256,192},{320,256},{384,320},{4... | collective-permute-start | bytes 884744 | tf_op jit(solution)/shard_map/ppermute | solution.py:68
  255.9 1.7 copy-start.3
  258.9 21.8 %all-to-all-start.2 = ((bf16[64,8,256]{2,1,0:T(8,128)(2,1)}), bf16[64,8,256]{2,1,0:T(8,128)(2,1)S(1)}, u32[]{:S(2)}, u32[]{:S(2)}) async-start(bf16[64,8,256]{2,1,0:T(8,128)(2,1)} %fusion.6), calls=%async_computation.3 | async-start | bytes 524288 | tf_op jit(solution)/shard_map/all_to_all | solution.py:97
  280.7 20.6 %all-to-all-start.1 = ((bf16[64,8,384]{2,1,0:T(8,128)(2,1)}), bf16[64,8,384]{2,1,0:T(8,128)(2,1)S(1)}, u32[]{:S(2)}, u32[]{:S(2)}) async-start(bf16[64,8,384]{2,1,0:T(8,128)(2,1)} %bitcast.16), calls=%async_computation.2 | async-start | bytes 786432 | tf_op jit(solution)/shard_map/all_to_all | solution.py:97
  287.2 2.4 copy-start.4
  289.6 12.7 %copy-start.5 = (bf16[32,512]{1,0:T(8,128)(2,1)S(1)}, bf16[32,512]{1,0:T(8,128)(2,1)}, u32[]{:S(2)}) copy-start(bf16[32,512]{1,0:T(8,128)(2,1)} %get-tuple-element.27) | copy-start | bytes 98308
Sparse Core Ops, SparseCore 0:
  49.3 89.9 reduce-scatter.1

commit v3 on v2

--- a/solution.py
+++ b/solution.py
@@ -54,66 +54,40 @@
     up_grad_part = (hidden_grad * silu_gate).astype(BF16)
     later_weight, _ = lax.optimization_barrier((pair_weight, part))
     flat_weight = later_weight.reshape(width, 2 * ff)
-
-    ranks = lax.axis_size("dp")
-    half = ranks // 2
-    same_parity = [[2 * i + q for i in range(half)] for q in range(2)]
-    to_right = [(i, (i + 1) % ranks) for i in range(ranks)]
-    to_left = [(i, (i - 1) % ranks) for i in range(ranks)]
-    is_even = lax.axis_index("dp") % 2 == 0
-
-    def gather(value):
-        own = lax.all_gather(value, "dp", axis=0, tiled=False, axis_index_groups=same_parity)
-        first = lax.ppermute(own[: half // 2], "dp", to_right)
-        second = lax.ppermute(own[half // 2 :], "dp", to_left)
-        other = jnp.concatenate([first, second], axis=0)
-        even = jnp.where(is_even, own, other)
-        odd = jnp.where(is_even, other, own)
-        return jnp.stack([even, odd], axis=1).reshape(slots, value.shape[1])
-
-    dot_hi = gate_dot.astype(BF16)
-    dot_lo = (gate_dot - dot_hi.astype(F32)).astype(BF16)
-    lane = jnp.arange(128)[None, :]
-    dots = jnp.where(lane == 0, dot_hi[:, None], jnp.where(lane == 1, dot_lo[:, None], jnp.zeros((), BF16)))
-    gathered = gather(jnp.concatenate([hidden, dots], axis=1))
-    hidden_full = gathered[:, :ff]
-    gate_grad_full = gather(gate_grad_part)
-    up_grad_full = gather(up_grad_part)
+    full = lax.all_gather(
+        jnp.concatenate([hidden, gate_grad_part, up_grad_part], axis=1), "dp", axis=0, tiled=True
+    )
+    hidden_full = full[:, :ff]
+    pair_full = full[:, ff:]
+    dots = lax.all_gather(gate_dot, "dp", axis=0, tiled=True)
+    dot_back = lax.all_to_all(
+        dots.reshape(experts, cap), "expert", split_axis=0, concat_axis=0, tiled=True
+    ).reshape(slots)
+    at_slot = place.astype(F32) * dot_back[None, :]
+    gate_grad = jnp.sum(jnp.where(named, at_slot[:, None, :], 0.0), axis=2) / gates
 
     expert_out = lax.dot_general(
         hidden_full, down_weight, (((1,), (1,)), ((), ())), preferred_element_type=F32
     ).astype(BF16)
-    row_grad = (
-        lax.dot_general(
-            gate_grad_full, flat_weight[:, :ff], (((1,), (1,)), ((), ())), preferred_element_type=F32
-        )
-        + lax.dot_general(
-            up_grad_full, flat_weight[:, ff:], (((1,), (1,)), ((), ())), preferred_element_type=F32
-        )
+    row_grad = lax.dot_general(
+        pair_full, flat_weight, (((1,), (1,)), ((), ())), preferred_element_type=F32
     ).astype(BF16)
-
-    def send_back(value):
-        sent = value.reshape(experts, cap, value.shape[1])
-        came = lax.all_to_all(sent, "expert", split_axis=0, concat_axis=0, tiled=True)
-        return came.reshape(slots, value.shape[1])
-
-    first_back = send_back(jnp.concatenate([expert_out, gathered[:, ff:]], axis=1))
-    grad_back = send_back(row_grad)
-    out_back = first_back[:, :width]
-    dot_back = jnp.sum(first_back[:, width:].astype(F32), axis=1)
-    at_slot = place.astype(F32) * dot_back[None, :]
-    gate_grad = jnp.sum(jnp.where(named, at_slot[:, None, :], 0.0), axis=2) / gates
+    back = jnp.concatenate([expert_out, row_grad], axis=1)
+    returned = lax.all_to_all(
+        back.reshape(experts, cap, 2 * width), "expert", split_axis=0, concat_axis=0, tiled=True
+    ).reshape(slots, 2 * width)
+    out_back = returned[:, :width]
+    grad_back = returned[:, width:]
 
     shares = counts.astype(F32) / jnp.sum(counts.astype(F32))
     slot_share = jnp.repeat(shares, cap)[:, None]
-    weighted_gate = (slot_share * gate_grad_full.astype(F32)).astype(BF16)
-    weighted_up = (slot_share * up_grad_full.astype(F32)).astype(BF16)
+    weighted_pair = (slot_share * pair_full.astype(F32)).astype(BF16)
     weighted_hidden = (slot_share * hidden_full.astype(F32)).astype(BF16)
     gate_update = lax.dot_general(
-        rows_in, weighted_gate, (((0,), (0,)), ((), ())), preferred_element_type=F32
+        rows_in, weighted_pair[:, :ff], (((0,), (0,)), ((), ())), preferred_element_type=F32
     ).astype(BF16)
     up_update = lax.dot_general(
-        rows_in, weighted_up, (((0,), (0,)), ((), ())), preferred_element_type=F32
+        rows_in, weighted_pair[:, ff:], (((0,), (0,)), ((), ())), preferred_element_type=F32
     ).astype(BF16)
     down_update = lax.dot_general(
         grad_rows, weighted_hidden, (((0,), (0,)), ((), ())), preferred_element_type=F32

time: 312 us -> 263 us (0.84)
  blocking collectives: 126 us -> 61.9 us
  waiting for transfers between devices: 106 us -> 134 us
  starting transfers between devices: 37.9 us -> 21.1 us
    all_gather x3 -> x0, blocking collectives: 92.4 us -> none  [gather(): lax.all_gather(value, 'dp', axis=0, tiled=False, axis_index_groups=same_p...]
    unnamed x0 -> x1, blocking collectives: none -> 28.4 us
    all_gather x0 -> x1, waiting for transfers between devices: none -> 26.8 us  [shards(): lax.all_gather(jnp.concatenate([hidden, gate_grad_part, up_grad_part], ax...]
    ppermute x6 -> x0, starting transfers between devices: 21.1 us -> none  [the longest x3 15.2 us: gather(): second = lax.ppermute(own[half // 2:], 'dp', to_left)]
    all_to_all x2, starting transfers between devices: 16.7 us -> 21 us  [the longest x1 10.6 us: shards(): lax.all_to_all(dots.reshape(experts, cap), 'expert', split_axis=0, concat...]
  transfers between devices with their start and end apart: 9 -> 4, of which waited for: 3 -> 4; matrix products, arithmetic and copies ran while one was open for 4% -> 4% of each run, Pallas kernels for 0% -> 0%
where the time goes in v3:
time: 263 us; the launch traced here: 260 us
  waiting for transfers between devices  134 us (51%)
  blocking collectives  61.9 us (24%)
  starting transfers between devices  21.1 us (8%)
  between operations  14.9 us (6%)
  other arithmetic  11.8 us (4%)
  matrix products  10.1 us (4%)
  local copies, waits for them, and re-layouts  6.45 us (2%)
    reduce_scatter x1, waiting for transfers between devices, shards(): sums = lax.psum_scatter(part, 'dp', scatter_dimension=0, tiled=True)  90.2 us
    all_to_all x1, blocking collectives, shards(): lax.all_to_all(outgoing, 'expert', split_axis=0, concat_axis=0, tiled=True)  33.5 us
    unnamed x1, blocking collectives  28.4 us
    all_gather x1, waiting for transfers between devices, shards(): lax.all_gather(jnp.concatenate([hidden, gate_grad_part, up_grad_part], ax...  26.8 us
    all_to_all x1, waiting for transfers between devices, shards(): lax.all_to_all(back.reshape(experts, cap, 2 * width), 'expert', split_axi...  10.7 us
    all_to_all x1, starting transfers between devices, shards(): lax.all_to_all(dots.reshape(experts, cap), 'expert', split_axis=0, concat...  10.6 us
    all_to_all x1, starting transfers between devices, shards(): lax.all_to_all(back.reshape(experts, cap, 2 * width), 'expert', split_axi...  10.4 us
    all_to_all x1, waiting for transfers between devices, shards(): lax.all_to_all(dots.reshape(experts, cap), 'expert', split_axis=0, concat...  6.47 us
  transfers between devices with their start and end apart: 4, of which 4 were waited for; matrix products, arithmetic and copies ran while one was open for 4% of the time, Pallas kernels for 0%

profile of v3, /device:TPU:6, one launch (start us, length us, event | category | flops | bytes accessed | tf_op | source)
XLA Modules:
  0.0 260.4 jit_solution(1140150477444870920)
XLA Ops:
  7.3 0.8 copy.24
  8.1 0.8 copy.23
  9.5 1.1 fusion.6
  10.6 33.5 %all_to_all.19 = bf16[64,8,512]{2,1,0:T(8,128)(2,1)S(1)} all-to-all(bf16[64,8,512]{2,1,0:T(8,128)(2,1)S(1)} %fusion.6), channel_id=1, replica_groups=mesh['dp'=16,'expert'=64] {'expert'}, dimensions={0} | all-to-all | bytes 1048576 | tf_op jit(solution)/shard_map/all_to_all | solution.py:35
  44.6 0.8 fusion.13
  45.4 3.2 %pad_maximum_fusion = f32[512,3,1024]{2,0,1:T(8,128)} fusion(f32[512,1,1024]{2,0,1:T(8,128)S(1)} %convolution_bitcast_fusion, f32[512,2,1024]{2,0,1:T(8,128)S(1)} %fusion.13), kind=kLoop, calls=%fused_computation | loop fusion | flops 1572864 | bytes 12582912 | tf_op jit(solution)/shard_map/concatenate | solution.py:44
  48.7 90.2 %reduce-scatter.2.cloned.1.call-done = f32[32,3,1024]{2,0,1:T(8,128)} async-done(((f32[512,3,1024]{2,0,1:T(8,128)}), f32[32,3,1024]{2,0,1:T(8,128)}) %reduce-scatter.2.cloned.1.call-update) | async-done | bytes 393232 | tf_op jit(solution)/shard_map/reduce_scatter | solution.py:45
  138.9 1.2 multiply_reduce_fusion
  140.1 0.7 pad_maximum_fusion.2
  140.9 1.3 dynamic-slice
  142.8 0.6 convert_reduce_fusion
  143.6 28.4 %all-reduce = f32[512]{0:T(512)S(1)} all-reduce(f32[512]{0:T(512)S(1)} %dynamic-update-slice), channel_id=1, replica_groups=mesh['dp'=16,'expert'=64] {'dp'}, use_global_device_ids=true, to_apply=%add | all-reduce | flops 512 | bytes 4096
  171.9 0.7 all_to_all.14
  172.6 10.6 %all-to-all-start.2 = ((f32[64,1,8]{2,1,0:T(1,128)}), f32[64,1,8]{2,1,0:T(1,128)S(1)}, u32[]{:S(2)}, u32[]{:S(2)}) async-start(f32[64,1,8]{2,1,0:T(1,128)} %bitcast.12), calls=%async_computation.3 | async-start | bytes 65536 | tf_op jit(solution)/shard_map/all_to_all | solution.py:63
  183.2 0.7 convert_divide_fusion
  184.3 6.5 %all-to-all-done.2 = f32[64,1,8]{2,1,0:T(1,128)S(1)} async-done(((f32[64,1,8]{2,1,0:T(1,128)}), f32[64,1,8]{2,1,0:T(1,128)S(1)}, u32[]{:S(2)}, u32[]{:S(2)}) %all-to-all-start.2) | async-done | bytes 2080 | tf_op jit(solution)/shard_map/all_to_all | solution.py:63
  190.8 0.5 broadcast.77
  191.3 0.7 reduce.3
  192.3 0.7 copy.29
  193.0 26.8 %all-gather.2.cloned.1.call-done = bf16[512,3072]{1,0:T(8,128)(2,1)} async-done(((bf16[32,3072]{1,0:T(8,128)(2,1)}), bf16[512,3072]{1,0:T(8,128)(2,1)}) %all-gather.2.cloned.1.call-update) | async-done | bytes 3145744 | tf_op jit(solution)/shard_map/all_gather | solution.py:57
  219.8 1.7 convolution_convert_fusion.3
  221.5 2.3 fusion.7
  223.9 1.0 copy.26
  224.9 10.4 %all-to-all-start.1 = ((bf16[64,8,512]{2,1,0:T(8,128)(2,1)}), bf16[64,8,512]{2,1,0:T(8,128)(2,1)S(1)}, u32[]{:S(2)}, u32[]{:S(2)}) async-start(bf16[64,8,512]{2,1,0:T(8,128)(2,1)} %bitcast.9), calls=%async_computation.2 | async-start | bytes 1048576 | tf_op jit(solution)/shard_map/all_to_all | solution.py:76
  235.3 2.0 multiply_convert_fusion
  237.3 0.5 fusion.4
  237.8 0.5 fusion.3
  238.3 1.8 fusion.5
  240.1 1.3 maximum_bitcast_fusion
  241.4 10.7 %all-to-all-done.1 = bf16[64,8,512]{2,1,0:T(8,128)(2,1)S(1)} async-done(((bf16[64,8,512]{2,1,0:T(8,128)(2,1)}), bf16[64,8,512]{2,1,0:T(8,128)(2,1)S(1)}, u32[]{:S(2)}, u32[]{:S(2)}) %all-to-all-start.1) | async-done | bytes 524320 | tf_op jit(solution)/shard_map/all_to_all | solution.py:76
  252.1 0.8 convolution_convert_fusion.4
  253.0 0.6 fusion.37
  (29 shorter events, 2.4 us)
Async XLA Ops:
  7.2 37.0 %copy-start = (bf16[1,256,1024]{2,1,0:T(8,128)(2,1)S(1)}, bf16[1,256,1024]{2,1,0:T(8,128)(2,1)}, u32[]{:S(2)}) copy-start(bf16[1,256,1024]{2,1,0:T(8,128)(2,1)} %param.12) | copy-start | bytes 1572868
  7.2 131.7 %reduce-scatter.2.cloned.1.call-start = ((), (), s32[]{:S(2)}) async-start(), calls=%async_computation.4 | async-start | bytes 6684672 | tf_op jit(solution)/shard_map/reduce_scatter | solution.py:45
  10.6 34.0 %copy-start.1 = (bf16[1,256,2,1024]{3,2,1,0:T(2,128)(2,1)S(1)}, bf16[1,256,2,1024]{3,2,1,0:T(2,128)(2,1)}, u32[]{:S(2)}) copy-start(bf16[1,256,2,1024]{3,2,1,0:T(2,128)(2,1)} %param.11) | copy-start | bytes 3145732
  48.6 94.2 %copy-start.2 = (s32[64]{0:T(128)S(1)}, s32[64]{0:T(128)}, u32[]{:S(2)}) copy-start(s32[64]{0:T(128)} %param.10) | copy-start | bytes 772
  48.6 171.2 %all-gather.2.cloned.1.call-start = ((), (), s32[]{:S(2)}) async-start(), calls=%async_computation.5 | async-start | bytes 3342336 | tf_op jit(solution)/shard_map/all_gather | solution.py:57
  172.6 18.2 %all-to-all-start.2 = ((f32[64,1,8]{2,1,0:T(1,128)}), f32[64,1,8]{2,1,0:T(1,128)S(1)}, u32[]{:S(2)}, u32[]{:S(2)}) async-start(f32[64,1,8]{2,1,0:T(1,128)} %bitcast.12), calls=%async_computation.3 | async-start | bytes 65536 | tf_op jit(solution)/shard_map/all_to_all | solution.py:63
  224.9 27.1 %all-to-all-start.1 = ((bf16[64,8,512]{2,1,0:T(8,128)(2,1)}), bf16[64,8,512]{2,1,0:T(8,128)(2,1)S(1)}, u32[]{:S(2)}, u32[]{:S(2)}) async-start(bf16[64,8,512]{2,1,0:T(8,128)(2,1)} %bitcast.9), calls=%async_computation.2 | async-start | bytes 1048576 | tf_op jit(solution)/shard_map/all_to_all | solution.py:76
Sparse Core Ops, SparseCore 0:
  48.8 90.1 reduce-scatter.1
  142.1 77.6 all-gather.1

commit v4 on v3

--- a/solution.py
+++ b/solution.py
@@ -54,30 +54,51 @@
     up_grad_part = (hidden_grad * silu_gate).astype(BF16)
     later_weight, _ = lax.optimization_barrier((pair_weight, part))
     flat_weight = later_weight.reshape(width, 2 * ff)
-    full = lax.all_gather(
-        jnp.concatenate([hidden, gate_grad_part, up_grad_part], axis=1), "dp", axis=0, tiled=True
+    pair_full = lax.all_gather(
+        jnp.concatenate([gate_grad_part, up_grad_part], axis=1), "dp", axis=0, tiled=True
     )
-    hidden_full = full[:, :ff]
-    pair_full = full[:, ff:]
-    dots = lax.all_gather(gate_dot, "dp", axis=0, tiled=True)
-    dot_back = lax.all_to_all(
-        dots.reshape(experts, cap), "expert", split_axis=0, concat_axis=0, tiled=True
-    ).reshape(slots)
+
+    ranks = lax.axis_size("dp")
+    side = 4
+    strided = [[q + side * i for i in range(ranks // side)] for q in range(side)]
+    nearby = [[side * i + q for q in range(side)] for i in range(ranks // side)]
+    dot_hi = gate_dot.astype(BF16)
+    dot_lo = (gate_dot - dot_hi.astype(F32)).astype(BF16)
+    lane = jnp.arange(128)[None, :]
+    dots = jnp.where(
+        lane == 0, dot_hi[:, None], jnp.where(lane == 1, dot_lo[:, None], jnp.zeros((), BF16))
+    )
+    payload = jnp.concatenate([hidden, dots], axis=1)
+    columns = lax.all_gather(payload, "dp", axis=0, tiled=True, axis_index_groups=strided)
+    cut = ff // 2
+
+    def near(value):
+        got = lax.all_gather(value, "dp", axis=0, tiled=False, axis_index_groups=nearby)
+        got = got.reshape(side, ranks // side, slots // ranks, value.shape[1])
+        return got.transpose(1, 0, 2, 3).reshape(slots, value.shape[1])
+
+    low = near(columns[:, :cut])
+    high = near(columns[:, cut:])
+    hidden_full = jnp.concatenate([low, high[:, : ff - cut]], axis=1)
+    expert_out = lax.dot_general(
+        hidden_full, down_weight, (((1,), (1,)), ((), ())), preferred_element_type=F32
+    ).astype(BF16)
+
+    def send_back(value):
+        sent = value.reshape(experts, cap, value.shape[1])
+        came = lax.all_to_all(sent, "expert", split_axis=0, concat_axis=0, tiled=True)
+        return came.reshape(slots, value.shape[1])
+
+    first_back = send_back(jnp.concatenate([expert_out, high[:, ff - cut :]], axis=1))
+    out_back = first_back[:, :width]
+    dot_back = jnp.sum(first_back[:, width:].astype(F32), axis=1)
     at_slot = place.astype(F32) * dot_back[None, :]
     gate_grad = jnp.sum(jnp.where(named, at_slot[:, None, :], 0.0), axis=2) / gates
 
-    expert_out = lax.dot_general(
-        hidden_full, down_weight, (((1,), (1,)), ((), ())), preferred_element_type=F32
-    ).astype(BF16)
     row_grad = lax.dot_general(
         pair_full, flat_weight, (((1,), (1,)), ((), ())), preferred_element_type=F32
     ).astype(BF16)
-    back = jnp.concatenate([expert_out, row_grad], axis=1)
-    returned = lax.all_to_all(
-        back.reshape(experts, cap, 2 * width), "expert", split_axis=0, concat_axis=0, tiled=True
-    ).reshape(slots, 2 * width)
-    out_back = returned[:, :width]
-    grad_back = returned[:, width:]
+    grad_back = send_back(row_grad)
 
     shares = counts.astype(F32) / jnp.sum(counts.astype(F32))
     slot_share = jnp.repeat(shares, cap)[:, None]

time: 263 us -> 260 us (0.989)
  blocking collectives: 61.9 us -> 91 us
  waiting for transfers between devices: 134 us -> 106 us
  starting transfers between devices: 21.1 us -> 17 us
    all_gather x0 -> x3, blocking collectives: none -> 57.5 us  [the longest x2 34.3 us: near(): lax.all_gather(value, 'dp', axis=0, tiled=False, axis_index_groups=nearby)]
    unnamed x1 -> x0, blocking collectives: 28.4 us -> none
    all_gather x1, waiting for transfers between devices: 26.8 us -> 0.01 us  [shards(): lax.all_gather(jnp.concatenate([gate_grad_part, up_grad_part], axis=1), '...]
    all_to_all x2, starting transfers between devices: 21 us -> 17 us  [send_back(): lax.all_to_all(sent, 'expert', split_axis=0, concat_axis=0, tiled=True)]
    unnamed x13 -> x37, local copies, waits for them, and re-layouts: 3.99 us -> 5.41 us
  transfers between devices with their start and end apart: 4 -> 4, of which waited for: 4 -> 3; matrix products, arithmetic and copies ran while one was open for 4% -> 6% of each run, Pallas kernels for 0% -> 0%
where the time goes in v4:
time: 260 us; the launch traced here: 258 us
  waiting for transfers between devices  106 us (41%)
  blocking collectives  91 us (35%)
  starting transfers between devices  17 us (7%)
  between operations  14.4 us (6%)
  other arithmetic  11 us (4%)
  matrix products  10.2 us (4%)
  local copies, waits for them, and re-layouts  8.64 us (3%)
    reduce_scatter x1, waiting for transfers between devices, shards(): sums = lax.psum_scatter(part, 'dp', scatter_dimension=0, tiled=True)  90 us
    all_gather x2, blocking collectives, near(): lax.all_gather(value, 'dp', axis=0, tiled=False, axis_index_groups=nearby)  34.3 us
    all_to_all x1, blocking collectives, shards(): lax.all_to_all(outgoing, 'expert', split_axis=0, concat_axis=0, tiled=True)  33.5 us
    all_gather x1, blocking collectives, shards(): lax.all_gather(payload, 'dp', axis=0, tiled=True, axis_index_groups=strided)  23.2 us
    all_to_all x2, starting transfers between devices, send_back(): lax.all_to_all(sent, 'expert', split_axis=0, concat_axis=0, tiled=True)  17 us
    all_to_all x2, waiting for transfers between devices, send_back(): lax.all_to_all(sent, 'expert', split_axis=0, concat_axis=0, tiled=True)  15.6 us
    unnamed x37, local copies, waits for them, and re-layouts  5.41 us
  transfers between devices with their start and end apart: 4, of which 3 were waited for; matrix products, arithmetic and copies ran while one was open for 6% of the time, Pallas kernels for 0%

profile of v4, /device:TPU:6, one launch (start us, length us, event | category | flops | bytes accessed | tf_op | source)
XLA Modules:
  0.0 257.9 jit_solution(12316758694703664391)
XLA Ops:
  7.3 0.8 copy.24
  8.1 0.8 copy.23
  9.3 0.8 fusion.36
  10.2 0.6 copy-done.5
  10.8 1.1 fusion.4
  11.9 33.5 %all_to_all.15 = bf16[64,8,512]{2,1,0:T(8,128)(2,1)S(1)} all-to-all(bf16[64,8,512]{2,1,0:T(8,128)(2,1)S(1)} %fusion.4), channel_id=1, replica_groups=mesh['dp'=16,'expert'=64] {'expert'}, dimensions={0} | all-to-all | bytes 1048576 | tf_op jit(solution)/shard_map/all_to_all | solution.py:35
  45.9 0.8 fusion.9
  46.6 3.2 %pad_maximum_fusion = f32[512,3,1024]{2,0,1:T(8,128)} fusion(f32[512,1,1024]{2,0,1:T(8,128)S(1)} %convolution_bitcast_fusion, f32[512,2,1024]{2,0,1:T(8,128)S(1)} %fusion.9), kind=kLoop, calls=%fused_computation | loop fusion | flops 1572864 | bytes 12582912 | tf_op jit(solution)/shard_map/concatenate | solution.py:44
  49.9 90.0 %reduce-scatter.2.cloned.1.call-done = f32[32,3,1024]{2,0,1:T(8,128)} async-done(((f32[512,3,1024]{2,0,1:T(8,128)}), f32[32,3,1024]{2,0,1:T(8,128)}) %reduce-scatter.2.cloned.1.call-update) | async-done | bytes 393232 | tf_op jit(solution)/shard_map/reduce_scatter | solution.py:45
  139.9 1.2 multiply_convert_fusion.4
  141.2 0.7 pad_maximum_fusion.5
  142.0 23.2 %all_gather.18 = bf16[128,1152]{1,0:T(8,128)(2,1)S(1)} all-gather(bf16[32,1152]{1,0:T(8,128)(2,1)S(1)} %pad_maximum_fusion.6), channel_id=1, replica_groups={{0,256,512,768},{64,320,576,832},{128,384,640,896},{192,448,704,960},{1..., dimensions={0}, use_global_device_ids=true | all-gather | bytes 368640 | tf_op jit(solution)/shard_map/all_gather | solution.py:72
  165.2 18.1 %all-gather.1 = bf16[512,640]{1,0:T(8,128)(2,1)S(1)} all-gather(bf16[128,640]{1,0:T(8,128)(2,1)S(1)} %slice.66), channel_id=3, replica_groups={{0,64,128,192},{256,320,384,448},{512,576,640,704},{768,832,896,960},{1..., dimensions={0}, use_global_device_ids=true | all-gather | bytes 819200 | tf_op jit(solution)/shard_map/all_gather | solution.py:76
  183.5 0.8 copy.32
  184.3 16.1 %all-gather = bf16[512,512]{1,0:T(8,128)(2,1)S(1)} all-gather(bf16[128,512]{1,0:T(8,128)(2,1)S(1)} %slice.65), channel_id=2, replica_groups={{0,64,128,192},{256,320,384,448},{512,576,640,704},{768,832,896,960},{1..., dimensions={0}, use_global_device_ids=true | all-gather | bytes 655360 | tf_op jit(solution)/shard_map/all_gather | solution.py:76
  200.5 0.5 convolution_convert_fusion.4
  201.4 0.9 copy.29
  202.3 10.3 %all-to-all-start.1 = ((bf16[64,8,384]{2,1,0:T(8,128)(2,1)}), bf16[64,8,384]{2,1,0:T(8,128)(2,1)S(1)}, u32[]{:S(2)}, u32[]{:S(2)}) async-start(bf16[64,8,384]{2,1,0:T(8,128)(2,1)} %bitcast.16), calls=%async_computation.2 | async-start | bytes 786432 | tf_op jit(solution)/shard_map/all_to_all | solution.py:89
  212.6 1.3 convert_reduce_fusion.1
  213.8 1.3 convert_divide_fusion
  215.1 0.7 broadcast_in_dim.124
  215.8 1.4 mul.68
  217.3 1.2 copy.33
  218.6 1.4 fusion.3
  219.9 6.8 %all-to-all-done.1 = bf16[64,8,384]{2,1,0:T(8,128)(2,1)S(1)} async-done(((bf16[64,8,384]{2,1,0:T(8,128)(2,1)}), bf16[64,8,384]{2,1,0:T(8,128)(2,1)S(1)}, u32[]{:S(2)}, u32[]{:S(2)}) %all-to-all-start.1) | async-done | bytes 393248 | tf_op jit(solution)/shard_map/all_to_all | solution.py:89
  227.1 0.7 copy.31
  227.9 0.6 fusion.31
  228.6 3.4 %fusion.5 = bf16[64,8,256]{2,1,0:T(8,128)(2,1)} fusion(bf16[512,2048]{1,0:T(8,128)(2,1)} %all-gather.4.cloned.1.call-done, bf16[256,2048]{1,0:T(8,128)(2,1)} %bitcast.85), kind=kOutput, calls=%fused_computation.16 | convolution fusion | flops 537001984 | bytes 3407872 | tf_op jit(solution)/shard_map/dot_general | solution.py:98
  232.0 6.7 %all-to-all-start.2 = ((bf16[64,8,256]{2,1,0:T(8,128)(2,1)}), bf16[64,8,256]{2,1,0:T(8,128)(2,1)S(1)}, u32[]{:S(2)}, u32[]{:S(2)}) async-start(bf16[64,8,256]{2,1,0:T(8,128)(2,1)} %fusion.5), calls=%async_computation.3 | async-start | bytes 524288 | tf_op jit(solution)/shard_map/all_to_all | solution.py:89
  240.2 1.3 maximum_bitcast_fusion
  241.5 8.8 %all-to-all-done.2 = bf16[64,8,256]{2,1,0:T(8,128)(2,1)S(1)} async-done(((bf16[64,8,256]{2,1,0:T(8,128)(2,1)}), bf16[64,8,256]{2,1,0:T(8,128)(2,1)S(1)}, u32[]{:S(2)}, u32[]{:S(2)}) %all-to-all-start.2) | async-done | bytes 262176 | tf_op jit(solution)/shard_map/all_to_all | solution.py:89
  250.3 0.8 convolution_convert_fusion.5
  (62 shorter events, 3.7 us)
Async XLA Ops:
  7.2 38.2 %copy-start = (bf16[1,256,1024]{2,1,0:T(8,128)(2,1)S(1)}, bf16[1,256,1024]{2,1,0:T(8,128)(2,1)}, u32[]{:S(2)}) copy-start(bf16[1,256,1024]{2,1,0:T(8,128)(2,1)} %param.12) | copy-start | bytes 1572868
  7.2 132.8 %reduce-scatter.2.cloned.1.call-start = ((), (), s32[]{:S(2)}) async-start(), calls=%async_computation.4 | async-start | bytes 6684672 | tf_op jit(solution)/shard_map/reduce_scatter | solution.py:45
  7.2 1.9 copy-start.10
  8.1 1.0 copy-start.8
  10.2 0.6 copy-start.5
  11.8 34.0 %copy-start.1 = (bf16[1,256,2,1024]{3,2,1,0:T(2,128)(2,1)S(1)}, bf16[1,256,2,1024]{3,2,1,0:T(2,128)(2,1)}, u32[]{:S(2)}) copy-start(bf16[1,256,2,1024]{3,2,1,0:T(2,128)(2,1)} %param.11) | copy-start | bytes 3145732
  49.9 178.7 %all-gather.4.cloned.1.call-start = ((), (), s32[]{:S(2)}) async-start(), calls=%async_computation.5 | async-start | bytes 2228224 | tf_op jit(solution)/shard_map/all_gather | solution.py:57
  200.4 0.9 copy-start.3
  202.3 24.4 %all-to-all-start.1 = ((bf16[64,8,384]{2,1,0:T(8,128)(2,1)}), bf16[64,8,384]{2,1,0:T(8,128)(2,1)S(1)}, u32[]{:S(2)}, u32[]{:S(2)}) async-start(bf16[64,8,384]{2,1,0:T(8,128)(2,1)} %bitcast.16), calls=%async_computation.2 | async-start | bytes 786432 | tf_op jit(solution)/shard_map/all_to_all | solution.py:89
  217.3 1.3 copy-start.14
  218.5 8.3 %copy-start.6 = (bf16[32,512]{1,0:T(8,128)(2,1)S(1)}, bf16[32,512]{1,0:T(8,128)(2,1)}, u32[]{:S(2)}) copy-start(bf16[32,512]{1,0:T(8,128)(2,1)} %copy-done.5) | copy-start | bytes 98308
  218.5 8.3 %copy-start.11 = (s32[512]{0:T(512)S(1)}, s32[512]{0:T(512)}, u32[]{:S(2)}) copy-start(s32[512]{0:T(512)} %copy-done.10) | copy-start | bytes 6148
  218.5 8.5 %copy-start.9 = (f32[32,8]{1,0:T(8,128)S(1)}, f32[32,8]{1,0:T(8,128)}, u32[]{:S(2)}) copy-start(f32[32,8]{1,0:T(8,128)} %copy-done.8) | copy-start | bytes 3076
  218.5 9.2 %copy-start.12 = (bf16[32,512]{1,0:T(8,128)(2,1)S(1)}, bf16[32,512]{1,0:T(8,128)(2,1)}, u32[]{:S(2)}) copy-start(bf16[32,512]{1,0:T(8,128)(2,1)} %get-tuple-element.14) | copy-start | bytes 98308
  218.5 9.2 %copy-start.13 = (bf16[32,512]{1,0:T(8,128)(2,1)S(1)}, bf16[32,512]{1,0:T(8,128)(2,1)}, u32[]{:S(2)}) copy-start(bf16[32,512]{1,0:T(8,128)(2,1)} %get-tuple-element.15) | copy-start | bytes 98308
  228.6 10.1 %copy-start.2 = (bf16[512,2048]{1,0:T(8,128)(2,1)S(1)}, bf16[512,2048]{1,0:T(8,128)(2,1)}, u32[]{:S(2)}) copy-start(bf16[512,2048]{1,0:T(8,128)(2,1)} %all-gather.4.cloned.1.call-done) | copy-start | bytes 6291460
  228.6 10.1 %copy-start.15 = (f32[512]{0:T(512)S(1)}, f32[512]{0:T(512)}, u32[]{:S(2)}) copy-start(f32[512]{0:T(512)} %mul.68) | copy-start | bytes 6148
  232.0 18.2 %all-to-all-start.2 = ((bf16[64,8,256]{2,1,0:T(8,128)(2,1)}), bf16[64,8,256]{2,1,0:T(8,128)(2,1)S(1)}, u32[]{:S(2)}, u32[]{:S(2)}) async-start(bf16[64,8,256]{2,1,0:T(8,128)(2,1)} %fusion.5), calls=%async_computation.3 | async-start | bytes 524288 | tf_op jit(solution)/shard_map/all_to_all | solution.py:89
  239.1 1.0 copy-start.4
  240.2 10.1 %copy-start.7 = (bf16[32,512]{1,0:T(8,128)(2,1)S(1)}, bf16[32,512]{1,0:T(8,128)(2,1)}, u32[]{:S(2)}) copy-start(bf16[32,512]{1,0:T(8,128)(2,1)} %copy-done.5) | copy-start | bytes 98308
Sparse Core Ops, SparseCore 0:
  50.0 89.8 reduce-scatter.1
  142.6 77.2 all-gather.3

commit v5 on v4

--- a/solution.py
+++ b/solution.py
@@ -43,6 +43,11 @@
     hidden_grad_part = jnp.dot(grad_rows, down_weight, preferred_element_type=F32)
     part = jnp.concatenate([pair_part, hidden_grad_part[:, None, :]], axis=1)
     sums = lax.psum_scatter(part, "dp", scatter_dimension=0, tiled=True)
+    later_weight, later_counts, _ = lax.optimization_barrier((pair_weight, counts, part))
+    flat_weight = later_weight.reshape(width, 2 * ff)
+    shares = later_counts.astype(F32) / jnp.sum(later_counts.astype(F32))
+    slot_share = jnp.repeat(shares, cap)[:, None]
+    sums, flat_weight, slot_share = lax.optimization_barrier((sums, flat_weight, slot_share))
     gate_part, up_part, hidden_grad = sums[:, 0], sums[:, 1], sums[:, 2]
     sig_gate = jax.nn.sigmoid(gate_part)
     silu_gate = gate_part * sig_gate
@@ -52,8 +57,6 @@
     hidden = hidden_value.astype(BF16)
     gate_grad_part = (hidden_grad * up_part * slope_term).astype(BF16)
     up_grad_part = (hidden_grad * silu_gate).astype(BF16)
-    later_weight, _ = lax.optimization_barrier((pair_weight, part))
-    flat_weight = later_weight.reshape(width, 2 * ff)
     pair_full = lax.all_gather(
         jnp.concatenate([gate_grad_part, up_grad_part], axis=1), "dp", axis=0, tiled=True
     )
@@ -90,18 +93,16 @@
         return came.reshape(slots, value.shape[1])
 
     first_back = send_back(jnp.concatenate([expert_out, high[:, ff - cut :]], axis=1))
+    row_grad = lax.dot_general(
+        pair_full, flat_weight, (((1,), (1,)), ((), ())), preferred_element_type=F32
+    ).astype(BF16)
+    grad_back = send_back(row_grad)
+    first_back, pair_full, _ = lax.optimization_barrier((first_back, pair_full, row_grad))
     out_back = first_back[:, :width]
     dot_back = jnp.sum(first_back[:, width:].astype(F32), axis=1)
     at_slot = place.astype(F32) * dot_back[None, :]
     gate_grad = jnp.sum(jnp.where(named, at_slot[:, None, :], 0.0), axis=2) / gates
 
-    row_grad = lax.dot_general(
-        pair_full, flat_weight, (((1,), (1,)), ((), ())), preferred_element_type=F32
-    ).astype(BF16)
-    grad_back = send_back(row_grad)
-
-    shares = counts.astype(F32) / jnp.sum(counts.astype(F32))
-    slot_share = jnp.repeat(shares, cap)[:, None]
     weighted_pair = (slot_share * pair_full.astype(F32)).astype(BF16)
     weighted_hidden = (slot_share * hidden_full.astype(F32)).astype(BF16)
     gate_update = lax.dot_general(

time: 260 us -> 257 us (0.988)
    all_gather x1, waiting for transfers between devices: 0.01 us -> 6.22 us  [shards(): lax.all_gather(jnp.concatenate([gate_grad_part, up_grad_part], axis=1), '...]
    all_to_all x2, waiting for transfers between devices: 15.6 us -> 11.5 us  [send_back(): lax.all_to_all(sent, 'expert', split_axis=0, concat_axis=0, tiled=True)]
    reduce_scatter x1, waiting for transfers between devices: 90 us -> 86.8 us  [shards(): sums = lax.psum_scatter(part, 'dp', scatter_dimension=0, tiled=True)]
    unnamed x37 -> x33, local copies, waits for them, and re-layouts: 5.41 us -> 5.28 us
  transfers between devices with their start and end apart: 4 -> 4, of which waited for: 3 -> 4; matrix products, arithmetic and copies ran while one was open for 6% -> 5% of each run, Pallas kernels for 0% -> 0%
where the time goes in v5:
time: 257 us; the launch traced here: 255 us
  waiting for transfers between devices  105 us (41%)
  blocking collectives  91.2 us (35%)
  starting transfers between devices  18.2 us (7%)
  between operations  14.4 us (6%)
  other arithmetic  10.3 us (4%)
  matrix products  10.3 us (4%)
  local copies, waits for them, and re-layouts  6.56 us (3%)
    reduce_scatter x1, waiting for transfers between devices, shards(): sums = lax.psum_scatter(part, 'dp', scatter_dimension=0, tiled=True)  86.8 us
    all_gather x2, blocking collectives, near(): lax.all_gather(value, 'dp', axis=0, tiled=False, axis_index_groups=nearby)  34.6 us
    all_to_all x1, blocking collectives, shards(): lax.all_to_all(outgoing, 'expert', split_axis=0, concat_axis=0, tiled=True)  33.4 us
    all_gather x1, blocking collectives, shards(): lax.all_gather(payload, 'dp', axis=0, tiled=True, axis_index_groups=strided)  23.2 us
    all_to_all x2, starting transfers between devices, send_back(): lax.all_to_all(sent, 'expert', split_axis=0, concat_axis=0, tiled=True)  18.1 us
    all_to_all x2, waiting for transfers between devices, send_back(): lax.all_to_all(sent, 'expert', split_axis=0, concat_axis=0, tiled=True)  11.5 us
    all_gather x1, waiting for transfers between devices, shards(): lax.all_gather(jnp.concatenate([gate_grad_part, up_grad_part], axis=1), '...  6.22 us
    unnamed x33, local copies, waits for them, and re-layouts  5.28 us
  transfers between devices with their start and end apart: 4, of which 4 were waited for; matrix products, arithmetic and copies ran while one was open for 5% of the time, Pallas kernels for 0%

profile of v5, /device:TPU:6, one launch (start us, length us, event | category | flops | bytes accessed | tf_op | source)
XLA Modules:
  0.0 255.4 jit_solution(9457476217939288717)
XLA Ops:
  7.3 0.9 copy.23
  8.2 0.8 copy.24
  9.8 0.8 fusion.42
  10.6 0.6 copy-done.4
  11.2 1.1 fusion.4
  12.3 33.4 %all_to_all.15 = bf16[64,8,512]{2,1,0:T(8,128)(2,1)S(1)} all-to-all(bf16[64,8,512]{2,1,0:T(8,128)(2,1)S(1)} %fusion.4), channel_id=1, replica_groups=mesh['dp'=16,'expert'=64] {'expert'}, dimensions={0} | all-to-all | bytes 1048576 | tf_op jit(solution)/shard_map/all_to_all | solution.py:35
  45.7 0.8 fusion.8
  46.9 3.2 %pad_maximum_fusion = f32[512,3,1024]{2,0,1:T(8,128)} fusion(f32[512,1,1024]{2,0,1:T(8,128)S(1)} %convolution_bitcast_fusion, f32[512,2,1024]{2,0,1:T(8,128)S(1)} %fusion.8), kind=kLoop, calls=%fused_computation | loop fusion | flops 1572864 | bytes 12582912 | tf_op jit(solution)/shard_map/concatenate | solution.py:44
  50.2 0.6 copy-done.13
  50.8 0.6 convert_reduce_fusion.1
  51.4 0.6 convert_divide_fusion
  52.2 1.2 copy.33
  53.5 86.8 %reduce-scatter.2.cloned.1.call-done = f32[32,3,1024]{2,0,1:T(8,128)} async-done(((f32[512,3,1024]{2,0,1:T(8,128)}), f32[32,3,1024]{2,0,1:T(8,128)}) %reduce-scatter.2.cloned.1.call-update) | async-done | bytes 393232 | tf_op jit(solution)/shard_map/reduce_scatter | solution.py:45
  140.3 1.2 fusion.26
  141.5 0.7 pad_maximum_fusion.5
  142.4 23.2 %all_gather.18 = bf16[128,1152]{1,0:T(8,128)(2,1)S(1)} all-gather(bf16[32,1152]{1,0:T(8,128)(2,1)S(1)} %pad_maximum_fusion.6), channel_id=1, replica_groups={{0,256,512,768},{64,320,576,832},{128,384,640,896},{192,448,704,960},{1..., dimensions={0}, use_global_device_ids=true | all-gather | bytes 368640 | tf_op jit(solution)/shard_map/all_gather | solution.py:75
  165.6 18.2 %all-gather.1 = bf16[512,640]{1,0:T(8,128)(2,1)S(1)} all-gather(bf16[128,640]{1,0:T(8,128)(2,1)S(1)} %slice.63), channel_id=3, replica_groups={{0,64,128,192},{256,320,384,448},{512,576,640,704},{768,832,896,960},{1..., dimensions={0}, use_global_device_ids=true | all-gather | bytes 819200 | tf_op jit(solution)/shard_map/all_gather | solution.py:79
  184.0 16.3 %all-gather = bf16[512,512]{1,0:T(8,128)(2,1)S(1)} all-gather(bf16[128,512]{1,0:T(8,128)(2,1)S(1)} %slice.62), channel_id=2, replica_groups={{0,64,128,192},{256,320,384,448},{512,576,640,704},{768,832,896,960},{1..., dimensions={0}, use_global_device_ids=true | all-gather | bytes 655360 | tf_op jit(solution)/shard_map/all_gather | solution.py:79
  200.5 0.5 convolution_convert_fusion.4
  201.0 0.9 copy.29
  201.9 10.5 %all-to-all-start.1 = ((bf16[64,8,384]{2,1,0:T(8,128)(2,1)}), bf16[64,8,384]{2,1,0:T(8,128)(2,1)S(1)}, u32[]{:S(2)}, u32[]{:S(2)}) async-start(bf16[64,8,384]{2,1,0:T(8,128)(2,1)} %bitcast.16), calls=%async_computation.2 | async-start | bytes 786432 | tf_op jit(solution)/shard_map/all_to_all | solution.py:92
  212.4 1.4 fusion.3
  213.8 6.2 %all-gather.4.cloned.1.call-done = bf16[512,2048]{1,0:T(8,128)(2,1)} async-done(((bf16[32,2048]{1,0:T(8,128)(2,1)}), bf16[512,2048]{1,0:T(8,128)(2,1)}) %all-gather.4.cloned.1.call-update) | async-done | bytes 2097168 | tf_op jit(solution)/shard_map/all_gather | solution.py:60
  220.0 3.5 %convolution_convert_fusion.3 = bf16[512,256]{1,0:T(8,128)(2,1)} fusion(bf16[512,2048]{1,0:T(8,128)(2,1)} %all-gather.4.cloned.1.call-done, bf16[256,2048]{1,0:T(8,128)(2,1)} %bitcast.100), kind=kOutput, calls=%fused_computation.14 | convolution fusion | flops 537001984 | bytes 3407872 | tf_op jit(solution)/shard_map/dot_general | solution.py:96
  223.5 3.1 %all-to-all-done.1 = bf16[64,8,384]{2,1,0:T(8,128)(2,1)S(1)} async-done(((bf16[64,8,384]{2,1,0:T(8,128)(2,1)}), bf16[64,8,384]{2,1,0:T(8,128)(2,1)S(1)}, u32[]{:S(2)}, u32[]{:S(2)}) %all-to-all-start.1) | async-done | bytes 393248 | tf_op jit(solution)/shard_map/all_to_all | solution.py:92
  226.6 1.1 multiply_convert_fusion
  228.7 7.6 %all-to-all-start.2 = ((bf16[64,8,256]{2,1,0:T(8,128)(2,1)}), bf16[64,8,256]{2,1,0:T(8,128)(2,1)S(1)}, u32[]{:S(2)}, u32[]{:S(2)}) async-start(bf16[64,8,256]{2,1,0:T(8,128)(2,1)} %bitcast.18), calls=%async_computation.3 | async-start | bytes 524288 | tf_op jit(solution)/shard_map/all_to_all | solution.py:92
  236.4 1.3 maximum_bitcast_fusion
  237.9 0.7 copy.31
  238.8 0.6 fusion.37
  239.4 8.4 %all-to-all-done.2 = bf16[64,8,256]{2,1,0:T(8,128)(2,1)S(1)} async-done(((bf16[64,8,256]{2,1,0:T(8,128)(2,1)}), bf16[64,8,256]{2,1,0:T(8,128)(2,1)S(1)}, u32[]{:S(2)}, u32[]{:S(2)}) %all-to-all-start.2) | async-done | bytes 262176 | tf_op jit(solution)/shard_map/all_to_all | solution.py:92
  247.8 0.8 convolution_convert_fusion.5
  (58 shorter events, 3.4 us)
Async XLA Ops:
  7.2 39.3 %copy-start = (bf16[1,256,1024]{2,1,0:T(8,128)(2,1)S(1)}, bf16[1,256,1024]{2,1,0:T(8,128)(2,1)}, u32[]{:S(2)}) copy-start(bf16[1,256,1024]{2,1,0:T(8,128)(2,1)} %param.12) | copy-start | bytes 1572868
  7.2 38.5 %copy-start.1 = (bf16[1,256,2,1024]{3,2,1,0:T(2,128)(2,1)S(1)}, bf16[1,256,2,1024]{3,2,1,0:T(2,128)(2,1)}, u32[]{:S(2)}) copy-start(bf16[1,256,2,1024]{3,2,1,0:T(2,128)(2,1)} %param.11) | copy-start | bytes 3145732
  7.2 133.1 %reduce-scatter.2.cloned.1.call-start = ((), (), s32[]{:S(2)}) async-start(), calls=%async_computation.4 | async-start | bytes 6684672 | tf_op jit(solution)/shard_map/reduce_scatter | solution.py:45
  7.2 1.9 copy-start.8
  8.9 0.6 copy-start.6
  10.6 0.6 copy-start.4
  50.1 0.7 copy-start.13
  50.2 169.8 %all-gather.4.cloned.1.call-start = ((), (), s32[]{:S(2)}) async-start(), calls=%async_computation.5 | async-start | bytes 2228224 | tf_op jit(solution)/shard_map/all_gather | solution.py:60
  52.2 160.2 %copy-start.12 = (f32[512,1]{0,1:T(1,128)}, f32[512,1]{0,1:T(1,128)S(1)}, u32[]{:S(2)}) copy-start(f32[512,1]{0,1:T(1,128)S(1)} %broadcast_in_dim_reshape.3) | copy-start | bytes 6148
  201.9 24.6 %all-to-all-start.1 = ((bf16[64,8,384]{2,1,0:T(8,128)(2,1)}), bf16[64,8,384]{2,1,0:T(8,128)(2,1)S(1)}, u32[]{:S(2)}, u32[]{:S(2)}) async-start(bf16[64,8,384]{2,1,0:T(8,128)(2,1)} %bitcast.16), calls=%async_computation.2 | async-start | bytes 786432 | tf_op jit(solution)/shard_map/all_to_all | solution.py:92
  220.0 6.6 %copy-start.2 = (bf16[512,2048]{1,0:T(8,128)(2,1)S(1)}, bf16[512,2048]{1,0:T(8,128)(2,1)}, u32[]{:S(2)}) copy-start(bf16[512,2048]{1,0:T(8,128)(2,1)} %all-gather.4.cloned.1.call-done) | copy-start | bytes 6291460
  227.6 8.7 %copy-start.5 = (bf16[32,512]{1,0:T(8,128)(2,1)S(1)}, bf16[32,512]{1,0:T(8,128)(2,1)}, u32[]{:S(2)}) copy-start(bf16[32,512]{1,0:T(8,128)(2,1)} %copy-done.4) | copy-start | bytes 98308
  227.7 8.7 %copy-start.3 = (bf16[256,1,1024]{2,0,1:T(8,128)(2,1)S(1)}, bf16[256,1,1024]{2,0,1:T(8,128)(2,1)}, u32[]{:S(2)}) copy-start(bf16[256,1,1024]{2,0,1:T(8,128)(2,1)} %fusion.3) | copy-start | bytes 1572868
  228.6 9.1 %copy-start.9 = (s32[512]{0:T(512)S(1)}, s32[512]{0:T(512)}, u32[]{:S(2)}) copy-start(s32[512]{0:T(512)} %copy-done.8) | copy-start | bytes 6148
  228.6 9.3 %copy-start.7 = (f32[32,8]{1,0:T(8,128)S(1)}, f32[32,8]{1,0:T(8,128)}, u32[]{:S(2)}) copy-start(f32[32,8]{1,0:T(8,128)} %copy-done.6) | copy-start | bytes 3076
  228.6 10.0 %copy-start.10 = (bf16[32,512]{1,0:T(8,128)(2,1)S(1)}, bf16[32,512]{1,0:T(8,128)(2,1)}, u32[]{:S(2)}) copy-start(bf16[32,512]{1,0:T(8,128)(2,1)} %get-tuple-element.26) | copy-start | bytes 98308
  228.6 10.0 %copy-start.11 = (bf16[32,512]{1,0:T(8,128)(2,1)S(1)}, bf16[32,512]{1,0:T(8,128)(2,1)}, u32[]{:S(2)}) copy-start(bf16[32,512]{1,0:T(8,128)(2,1)} %get-tuple-element.27) | copy-start | bytes 98308
  228.7 19.2 %all-to-all-start.2 = ((bf16[64,8,256]{2,1,0:T(8,128)(2,1)}), bf16[64,8,256]{2,1,0:T(8,128)(2,1)S(1)}, u32[]{:S(2)}, u32[]{:S(2)}) async-start(bf16[64,8,256]{2,1,0:T(8,128)(2,1)} %bitcast.18), calls=%async_computation.3 | async-start | bytes 524288 | tf_op jit(solution)/shard_map/all_to_all | solution.py:92
Sparse Core Ops, SparseCore 0:
  50.3 89.9 reduce-scatter.1
  143.0 76.9 all-gather.3

commit v6 on v5

--- a/solution.py
+++ b/solution.py
@@ -40,15 +40,34 @@
     pair_part = lax.dot_general(
         rows_in, pair_weight, (((1,), (0,)), ((), ())), preferred_element_type=F32
     )
-    hidden_grad_part = jnp.dot(grad_rows, down_weight, preferred_element_type=F32)
-    part = jnp.concatenate([pair_part, hidden_grad_part[:, None, :]], axis=1)
-    sums = lax.psum_scatter(part, "dp", scatter_dimension=0, tiled=True)
-    later_weight, later_counts, _ = lax.optimization_barrier((pair_weight, counts, part))
+    sums = lax.psum_scatter(pair_part, "dp", scatter_dimension=0, tiled=True)
+
+    ranks = lax.axis_size("dp")
+    side = 4
+    far = ranks // side
+    strided = [[q + side * i for i in range(far)] for q in range(side)]
+    nearby = [[side * i + q for q in range(side)] for i in range(far)]
+
+    hidden_grad_part = jnp.dot(grad_rows, down_weight, preferred_element_type=F32).astype(BF16)
+    blocks = hidden_grad_part.reshape(far, side, slots // ranks, ff).transpose(1, 0, 2, 3)
+    close = lax.all_to_all(
+        blocks, "dp", split_axis=0, concat_axis=0, axis_index_groups=nearby, tiled=True
+    )
+    close = close.astype(F32)
+    close = ((close[0] + close[1]) + (close[2] + close[3])).astype(BF16)
+    wide = lax.all_to_all(
+        close, "dp", split_axis=0, concat_axis=0, axis_index_groups=strided, tiled=True
+    )
+    hidden_grad = jnp.sum(wide.astype(F32), axis=0)
+
+    later_weight, later_counts, _ = lax.optimization_barrier((pair_weight, counts, pair_part))
     flat_weight = later_weight.reshape(width, 2 * ff)
     shares = later_counts.astype(F32) / jnp.sum(later_counts.astype(F32))
     slot_share = jnp.repeat(shares, cap)[:, None]
-    sums, flat_weight, slot_share = lax.optimization_barrier((sums, flat_weight, slot_share))
-    gate_part, up_part, hidden_grad = sums[:, 0], sums[:, 1], sums[:, 2]
+    sums, flat_weight, slot_share, hidden_grad = lax.optimization_barrier(
+        (sums, flat_weight, slot_share, hidden_grad)
+    )
+    gate_part, up_part = sums[:, 0], sums[:, 1]
     sig_gate = jax.nn.sigmoid(gate_part)
     silu_gate = gate_part * sig_gate
     hidden_value = silu_gate * up_part
@@ -61,10 +80,6 @@
         jnp.concatenate([gate_grad_part, up_grad_part], axis=1), "dp", axis=0, tiled=True
     )
 
-    ranks = lax.axis_size("dp")
-    side = 4
-    strided = [[q + side * i for i in range(ranks // side)] for q in range(side)]
-    nearby = [[side * i + q for q in range(side)] for i in range(ranks // side)]
     dot_hi = gate_dot.astype(BF16)
     dot_lo = (gate_dot - dot_hi.astype(F32)).astype(BF16)
     lane = jnp.arange(128)[None, :]
@@ -77,7 +92,7 @@
 
     def near(value):
         got = lax.all_gather(value, "dp", axis=0, tiled=False, axis_index_groups=nearby)
-        got = got.reshape(side, ranks // side, slots // ranks, value.shape[1])
+        got = got.reshape(side, far, slots // ranks, value.shape[1])
         return got.transpose(1, 0, 2, 3).reshape(slots, value.shape[1])
 
     low = near(columns[:, :cut])
@@ -97,7 +112,8 @@
         pair_full, flat_weight, (((1,), (1,)), ((), ())), preferred_element_type=F32
     ).astype(BF16)
     grad_back = send_back(row_grad)
-    first_back, pair_full, _ = lax.optimization_barrier((first_back, pair_full, row_grad))
+    first_back, _ = lax.optimization_barrier((first_back, row_grad))
+    pair_full, _ = lax.optimization_barrier((pair_full, row_grad))
     out_back = first_back[:, :width]
     dot_back = jnp.sum(first_back[:, width:].astype(F32), axis=1)
     at_slot = place.astype(F32) * dot_back[None, :]

time: 257 us -> 261 us (1.016)
  waiting for transfers between devices: 105 us -> 61.7 us
  blocking collectives: 91.2 us -> 127 us
  starting transfers between devices: 18.2 us -> 30 us
  other arithmetic: 10.3 us -> 7.43 us
    reduce_scatter x1, waiting for transfers between devices: 86.8 us -> 25 us  [shards(): sums = lax.psum_scatter(pair_part, 'dp', scatter_dimension=0, tiled=True)]
    all_to_all x0 -> x1, blocking collectives: none -> 35.5 us  [shards(): lax.all_to_all(blocks, 'dp', split_axis=0, concat_axis=0, axis_index_grou...]
    all_to_all x0 -> x1, waiting for transfers between devices: none -> 20.8 us  [shards(): lax.all_to_all(close, 'dp', split_axis=0, concat_axis=0, axis_index_group...]
    all_to_all x0 -> x1, starting transfers between devices: none -> 15.8 us  [shards(): lax.all_to_all(close, 'dp', split_axis=0, concat_axis=0, axis_index_group...]
    all_to_all x2, starting transfers between devices: 18.1 us -> 14.2 us  [send_back(): lax.all_to_all(sent, 'expert', split_axis=0, concat_axis=0, tiled=True)]
    all_gather x1, waiting for transfers between devices: 6.22 us -> 2.94 us  [shards(): lax.all_gather(jnp.concatenate([gate_grad_part, up_grad_part], axis=1), '...]
    concatenate x1 -> x0, other arithmetic: 3.23 us -> none  [shards(): part = jnp.concatenate([pair_part, hidden_grad_part[:, None, :]], axis=1)]
    unnamed x33 -> x35, local copies, waits for them, and re-layouts: 5.28 us -> 4.81 us
  transfers between devices with their start and end apart: 4 -> 5, of which waited for: 4 -> 5; matrix products, arithmetic and copies ran while one was open for 5% -> 6% of each run, Pallas kernels for 0% -> 0%
where the time goes in v6:
time: 261 us; the launch traced here: 259 us
  blocking collectives  127 us (49%)
  waiting for transfers between devices  61.7 us (24%)
  starting transfers between devices  30 us (11%)
  between operations  14.4 us (6%)
  matrix products  12.6 us (5%)
  other arithmetic  7.43 us (3%)
  local copies, waits for them, and re-layouts  6.73 us (3%)
    all_gather x2, blocking collectives, near(): lax.all_gather(value, 'dp', axis=0, tiled=False, axis_index_groups=nearby)  35.6 us
    all_to_all x1, blocking collectives, shards(): lax.all_to_all(blocks, 'dp', split_axis=0, concat_axis=0, axis_index_grou...  35.5 us
    all_to_all x1, blocking collectives, shards(): lax.all_to_all(outgoing, 'expert', split_axis=0, concat_axis=0, tiled=True)  33.4 us
    reduce_scatter x1, waiting for transfers between devices, shards(): sums = lax.psum_scatter(pair_part, 'dp', scatter_dimension=0, tiled=True)  25 us
    all_gather x1, blocking collectives, shards(): lax.all_gather(payload, 'dp', axis=0, tiled=True, axis_index_groups=strided)  22 us
    all_to_all x1, waiting for transfers between devices, shards(): lax.all_to_all(close, 'dp', split_axis=0, concat_axis=0, axis_index_group...  20.8 us
    all_to_all x1, starting transfers between devices, shards(): lax.all_to_all(close, 'dp', split_axis=0, concat_axis=0, axis_index_group...  15.8 us
    all_to_all x2, starting transfers between devices, send_back(): lax.all_to_all(sent, 'expert', split_axis=0, concat_axis=0, tiled=True)  14.2 us
  transfers between devices with their start and end apart: 5, of which 5 were waited for; matrix products, arithmetic and copies ran while one was open for 6% of the time, Pallas kernels for 0%

profile of v6, /device:TPU:6, one launch (start us, length us, event | category | flops | bytes accessed | tf_op | source)
XLA Modules:
  0.0 259.4 jit_solution(7619869913178570475)
XLA Ops:
  7.3 0.9 copy.31
  8.2 0.8 copy.32
  9.8 0.8 fusion.43
  10.6 0.6 copy-done.5
  11.2 1.1 fusion.4
  12.3 33.4 %all_to_all.25 = bf16[64,8,512]{2,1,0:T(8,128)(2,1)S(1)} all-to-all(bf16[64,8,512]{2,1,0:T(8,128)(2,1)S(1)} %fusion.4), channel_id=1, replica_groups=mesh['dp'=16,'expert'=64] {'expert'}, dimensions={0} | all-to-all | bytes 1048576 | tf_op jit(solution)/shard_map/all_to_all | solution.py:35
  45.7 2.7 %fusion.8 = f32[512,2,1024]{2,0,1:T(8,128)} fusion(bf16[256,2,1024]{2,1,0:T(2,128)(2,1)S(1)} %bitcast.87, bf16[512,512]{1,0:T(8,128)(2,1)S(1)} %bitcast.93), kind=kOutput, calls=%fused_computation.22 | convolution fusion | flops 536870912 | bytes 5505024 | tf_op jit(solution)/shard_map/dot_general | solution.py:40
  49.0 35.5 %all_to_all.26 = bf16[4,4,32,1024]{3,2,1,0:T(8,128)(2,1)S(1)} all-to-all(bf16[4,4,32,1024]{3,2,1,0:T(8,128)(2,1)S(1)} %bitcast.86), channel_id=1, replica_groups={{0,64,128,192},{256,320,384,448},{512,576,640,704},{768,832,896,960},{1..., dimensions={0} | all-to-all | bytes 2097152 | tf_op jit(solution)/shard_map/all_to_all | solution.py:53
  84.8 0.8 fusion.17
  85.6 15.8 %all-to-all-start.2 = ((bf16[4,32,1024]{2,1,0:T(8,128)(2,1)}), bf16[4,32,1024]{2,1,0:T(8,128)(2,1)S(1)}, u32[]{:S(2)}, u32[]{:S(2)}) async-start(bf16[4,32,1024]{2,1,0:T(8,128)(2,1)} %fusion.17), calls=%async_computation.3 | async-start | bytes 524288 | tf_op jit(solution)/shard_map/all_to_all | solution.py:58
  102.0 0.6 convert_divide_fusion
  102.7 0.7 broadcast_in_dim_reshape.3
  103.7 20.8 %all-to-all-done.2 = bf16[4,32,1024]{2,1,0:T(8,128)(2,1)S(1)} async-done(((bf16[4,32,1024]{2,1,0:T(8,128)(2,1)}), bf16[4,32,1024]{2,1,0:T(8,128)(2,1)S(1)}, u32[]{:S(2)}, u32[]{:S(2)}) %all-to-all-start.2) | async-done | bytes 262176 | tf_op jit(solution)/shard_map/all_to_all | solution.py:58
  124.5 25.0 %reduce-scatter.2.cloned.1.call-done = f32[32,2,1024]{2,0,1:T(8,128)} async-done(((f32[512,2,1024]{2,0,1:T(8,128)}), f32[32,2,1024]{2,0,1:T(8,128)}) %reduce-scatter.2.cloned.1.call-update) | async-done | bytes 262160 | tf_op jit(solution)/shard_map/reduce_scatter | solution.py:43
  149.5 1.2 fusion.28
  150.6 0.7 pad_maximum_fusion.4
  151.4 22.0 %all_gather.18 = bf16[128,1152]{1,0:T(8,128)(2,1)S(1)} all-gather(bf16[32,1152]{1,0:T(8,128)(2,1)S(1)} %pad_maximum_fusion.5), channel_id=1, replica_groups={{0,256,512,768},{64,320,576,832},{128,384,640,896},{192,448,704,960},{1..., dimensions={0}, use_global_device_ids=true | all-gather | bytes 368640 | tf_op jit(solution)/shard_map/all_gather | solution.py:90
  173.5 19.2 %all-gather.1 = bf16[512,640]{1,0:T(8,128)(2,1)S(1)} all-gather(bf16[128,640]{1,0:T(8,128)(2,1)S(1)} %slice.79), channel_id=3, replica_groups={{0,64,128,192},{256,320,384,448},{512,576,640,704},{768,832,896,960},{1..., dimensions={0}, use_global_device_ids=true | all-gather | bytes 819200 | tf_op jit(solution)/shard_map/all_gather | solution.py:94
  192.8 16.4 %all-gather = bf16[512,512]{1,0:T(8,128)(2,1)S(1)} all-gather(bf16[128,512]{1,0:T(8,128)(2,1)S(1)} %slice.78), channel_id=2, replica_groups={{0,64,128,192},{256,320,384,448},{512,576,640,704},{768,832,896,960},{1..., dimensions={0}, use_global_device_ids=true | all-gather | bytes 655360 | tf_op jit(solution)/shard_map/all_gather | solution.py:94
  209.3 0.8 copy.41
  211.0 0.9 copy.38
  211.9 7.5 %all-to-all-start.3 = ((bf16[64,8,384]{2,1,0:T(8,128)(2,1)}), bf16[64,8,384]{2,1,0:T(8,128)(2,1)S(1)}, u32[]{:S(2)}, u32[]{:S(2)}) async-start(bf16[64,8,384]{2,1,0:T(8,128)(2,1)} %bitcast.17), calls=%async_computation.4 | async-start | bytes 786432 | tf_op jit(solution)/shard_map/all_to_all | solution.py:107
  219.4 2.0 fusion.3
  221.5 2.9 %all-gather.4.cloned.1.call-done = bf16[512,2048]{1,0:T(8,128)(2,1)} async-done(((bf16[32,2048]{1,0:T(8,128)(2,1)}), bf16[512,2048]{1,0:T(8,128)(2,1)}) %all-gather.4.cloned.1.call-update) | async-done | bytes 2097168 | tf_op jit(solution)/shard_map/all_gather | solution.py:79
  224.4 3.2 %convolution_convert_fusion.4 = bf16[512,256]{1,0:T(8,128)(2,1)} fusion(bf16[512,2048]{1,0:T(8,128)(2,1)} %all-gather.4.cloned.1.call-done, bf16[256,2048]{1,0:T(8,128)(2,1)S(1)} %bitcast.98), kind=kOutput, calls=%fused_computation.13 | convolution fusion | flops 537001984 | bytes 3407872 | tf_op jit(solution)/shard_map/dot_general | solution.py:111
  229.0 4.6 %all-to-all-done.3 = bf16[64,8,384]{2,1,0:T(8,128)(2,1)S(1)} async-done(((bf16[64,8,384]{2,1,0:T(8,128)(2,1)}), bf16[64,8,384]{2,1,0:T(8,128)(2,1)S(1)}, u32[]{:S(2)}, u32[]{:S(2)}) %all-to-all-start.3) | async-done | bytes 393248 | tf_op jit(solution)/shard_map/all_to_all | solution.py:107
  233.6 6.7 %all-to-all-start.4 = ((bf16[64,8,256]{2,1,0:T(8,128)(2,1)}), bf16[64,8,256]{2,1,0:T(8,128)(2,1)S(1)}, u32[]{:S(2)}, u32[]{:S(2)}) async-start(bf16[64,8,256]{2,1,0:T(8,128)(2,1)} %bitcast.19), calls=%async_computation.5 | async-start | bytes 524288 | tf_op jit(solution)/shard_map/all_to_all | solution.py:107
  240.4 1.3 maximum_bitcast_fusion
  241.9 0.7 copy.40
  242.8 0.6 fusion.38
  243.4 8.4 %all-to-all-done.4 = bf16[64,8,256]{2,1,0:T(8,128)(2,1)S(1)} async-done(((bf16[64,8,256]{2,1,0:T(8,128)(2,1)}), bf16[64,8,256]{2,1,0:T(8,128)(2,1)S(1)}, u32[]{:S(2)}, u32[]{:S(2)}) %all-to-all-start.4) | async-done | bytes 262176 | tf_op jit(solution)/shard_map/all_to_all | solution.py:107
  251.8 0.8 convolution_convert_fusion.6
  (66 shorter events, 5.7 us)
Async XLA Ops:
  7.2 41.3 %copy-start = (bf16[1,256,1024]{2,1,0:T(8,128)(2,1)S(1)}, bf16[1,256,1024]{2,1,0:T(8,128)(2,1)}, u32[]{:S(2)}) copy-start(bf16[1,256,1024]{2,1,0:T(8,128)(2,1)} %param.12) | copy-start | bytes 1572868
  7.2 38.5 %copy-start.1 = (bf16[1,256,2,1024]{3,2,1,0:T(2,128)(2,1)S(1)}, bf16[1,256,2,1024]{3,2,1,0:T(2,128)(2,1)}, u32[]{:S(2)}) copy-start(bf16[1,256,2,1024]{3,2,1,0:T(2,128)(2,1)} %param.11) | copy-start | bytes 3145732
  7.2 142.3 %reduce-scatter.2.cloned.1.call-start = ((), (), s32[]{:S(2)}) async-start(), calls=%async_computation.6 | async-start | bytes 4456448 | tf_op jit(solution)/shard_map/reduce_scatter | solution.py:43
  7.3 1.9 copy-start.9
  8.9 0.6 copy-start.7
  10.6 0.6 copy-start.5
  84.8 16.6 %copy-start.14 = (s32[64]{0:T(128)S(1)}, s32[64]{0:T(128)}, u32[]{:S(2)}) copy-start(s32[64]{0:T(128)} %param.10) | copy-start | bytes 772
  85.6 38.8 %all-to-all-start.2 = ((bf16[4,32,1024]{2,1,0:T(8,128)(2,1)}), bf16[4,32,1024]{2,1,0:T(8,128)(2,1)S(1)}, u32[]{:S(2)}, u32[]{:S(2)}) async-start(bf16[4,32,1024]{2,1,0:T(8,128)(2,1)} %fusion.17), calls=%async_computation.3 | async-start | bytes 524288 | tf_op jit(solution)/shard_map/all_to_all | solution.py:58
  101.4 123.0 %all-gather.4.cloned.1.call-start = ((), (), s32[]{:S(2)}) async-start(), calls=%async_computation.7 | async-start | bytes 2228224 | tf_op jit(solution)/shard_map/all_gather | solution.py:79
  210.0 0.9 copy-start.3
  211.9 21.7 %all-to-all-start.3 = ((bf16[64,8,384]{2,1,0:T(8,128)(2,1)}), bf16[64,8,384]{2,1,0:T(8,128)(2,1)S(1)}, u32[]{:S(2)}, u32[]{:S(2)}) async-start(bf16[64,8,384]{2,1,0:T(8,128)(2,1)} %bitcast.17), calls=%async_computation.4 | async-start | bytes 786432 | tf_op jit(solution)/shard_map/all_to_all | solution.py:107
  221.5 6.1 %copy-start.13 = (f32[512,1]{0,1:T(1,128)S(1)}, f32[512,1]{0,1:T(1,128)}, u32[]{:S(2)}) copy-start(f32[512,1]{0,1:T(1,128)} %broadcast_in_dim_reshape.3) | copy-start | bytes 6148
  224.4 3.2 %copy-start.2 = (bf16[512,2048]{1,0:T(8,128)(2,1)S(1)}, bf16[512,2048]{1,0:T(8,128)(2,1)}, u32[]{:S(2)}) copy-start(bf16[512,2048]{1,0:T(8,128)(2,1)} %all-gather.4.cloned.1.call-done) | copy-start | bytes 6291460
  228.0 12.4 %copy-start.6 = (bf16[32,512]{1,0:T(8,128)(2,1)S(1)}, bf16[32,512]{1,0:T(8,128)(2,1)}, u32[]{:S(2)}) copy-start(bf16[32,512]{1,0:T(8,128)(2,1)} %copy-done.5) | copy-start | bytes 98308
  228.0 12.4 %copy-start.4 = (bf16[256,1,1024]{2,0,1:T(8,128)(2,1)S(1)}, bf16[256,1,1024]{2,0,1:T(8,128)(2,1)}, u32[]{:S(2)}) copy-start(bf16[256,1,1024]{2,0,1:T(8,128)(2,1)} %fusion.3) | copy-start | bytes 1572868
  229.0 12.7 %copy-start.10 = (s32[512]{0:T(512)S(1)}, s32[512]{0:T(512)}, u32[]{:S(2)}) copy-start(s32[512]{0:T(512)} %copy-done.9) | copy-start | bytes 6148
  229.0 12.9 %copy-start.8 = (f32[32,8]{1,0:T(8,128)S(1)}, f32[32,8]{1,0:T(8,128)}, u32[]{:S(2)}) copy-start(f32[32,8]{1,0:T(8,128)} %copy-done.7) | copy-start | bytes 3076
  229.0 13.6 %copy-start.11 = (bf16[32,512]{1,0:T(8,128)(2,1)S(1)}, bf16[32,512]{1,0:T(8,128)(2,1)}, u32[]{:S(2)}) copy-start(bf16[32,512]{1,0:T(8,128)(2,1)} %get-tuple-element.28) | copy-start | bytes 98308
  229.0 13.6 %copy-start.12 = (bf16[32,512]{1,0:T(8,128)(2,1)S(1)}, bf16[32,512]{1,0:T(8,128)(2,1)}, u32[]{:S(2)}) copy-start(bf16[32,512]{1,0:T(8,128)(2,1)} %get-tuple-element.29) | copy-start | bytes 98308
  233.6 18.2 %all-to-all-start.4 = ((bf16[64,8,256]{2,1,0:T(8,128)(2,1)}), bf16[64,8,256]{2,1,0:T(8,128)(2,1)S(1)}, u32[]{:S(2)}, u32[]{:S(2)}) async-start(bf16[64,8,256]{2,1,0:T(8,128)(2,1)} %bitcast.19), calls=%async_computation.5 | async-start | bytes 524288 | tf_op jit(solution)/shard_map/all_to_all | solution.py:107
Sparse Core Ops, SparseCore 0:
  48.6 100.8 reduce-scatter.1
  152.1 72.2 all-gather.3

commit v7 on v5

--- a/solution.py
+++ b/solution.py
@@ -17,20 +17,22 @@
     pair_weight = w_gate_up[0]
     down_weight = w_down[0]
 
-    slot_id = jnp.arange(slots, dtype=jnp.int32)
+    routes_by = routes.T
+    gates_by = gates.T
+    slot_id = jnp.arange(slots, dtype=jnp.int32)[:, None]
     slot_expert = slot_id // cap
-    slot_pos = slot_id % cap
-    named = routes[:, :, None] == slot_expert[None, None, :]
-    member = jnp.any(named, axis=1).astype(BF16)
-    earlier = jnp.tril(jnp.ones((rows, rows), BF16), -1)
-    before = jnp.dot(earlier, member, preferred_element_type=F32)
-    place = jnp.where(before == slot_pos[None, :].astype(F32), member, jnp.zeros((), BF16))
-    gate_of = jnp.sum(jnp.where(named, gates[:, :, None], 0.0), axis=1) * place.astype(F32)
-    gate_slot = jnp.sum(gate_of, axis=0)
+    slot_pos = (slot_id % cap).astype(F32)
+    named = routes_by[:, None, :] == slot_expert[None]
+    member = jnp.any(named, axis=0).astype(BF16)
+    earlier = jnp.triu(jnp.ones((rows, rows), BF16), 1)
+    before = jnp.dot(member, earlier, preferred_element_type=F32)
+    place = jnp.where(before == slot_pos, member, jnp.zeros((), BF16))
+    gate_of = jnp.sum(jnp.where(named, gates_by[:, None, :], 0.0), axis=0) * place.astype(F32)
+    gate_slot = jnp.sum(gate_of, axis=1, keepdims=True)
 
     both = jnp.concatenate([tokens, cotangent], axis=1)
-    picked = lax.dot_general(place, both, (((0,), (0,)), ((), ())), preferred_element_type=F32)
-    scale = jnp.where(jnp.arange(2 * width)[None, :] < width, 1.0, gate_slot[:, None])
+    picked = jnp.dot(place, both, preferred_element_type=F32)
+    scale = jnp.where(jnp.arange(2 * width)[None, :] < width, 1.0, gate_slot)
     outgoing = (picked * scale).astype(BF16).reshape(experts, cap, 2 * width)
     arrived = lax.all_to_all(outgoing, "expert", split_axis=0, concat_axis=0, tiled=True)
     arrived = arrived.reshape(slots, 2 * width)
@@ -44,7 +46,7 @@
     part = jnp.concatenate([pair_part, hidden_grad_part[:, None, :]], axis=1)
     sums = lax.psum_scatter(part, "dp", scatter_dimension=0, tiled=True)
     later_weight, later_counts, _ = lax.optimization_barrier((pair_weight, counts, part))
-    flat_weight = later_weight.reshape(width, 2 * ff)
+    flat_weight = later_weight.reshape(width, 2 * ff).T
     shares = later_counts.astype(F32) / jnp.sum(later_counts.astype(F32))
     slot_share = jnp.repeat(shares, cap)[:, None]
     sums, flat_weight, slot_share = lax.optimization_barrier((sums, flat_weight, slot_share))
@@ -93,15 +95,14 @@
         return came.reshape(slots, value.shape[1])
 
     first_back = send_back(jnp.concatenate([expert_out, high[:, ff - cut :]], axis=1))
-    row_grad = lax.dot_general(
-        pair_full, flat_weight, (((1,), (1,)), ((), ())), preferred_element_type=F32
-    ).astype(BF16)
+    row_grad = jnp.dot(pair_full, flat_weight, preferred_element_type=F32).astype(BF16)
     grad_back = send_back(row_grad)
-    first_back, pair_full, _ = lax.optimization_barrier((first_back, pair_full, row_grad))
+    first_back, _ = lax.optimization_barrier((first_back, row_grad))
+    pair_full, _ = lax.optimization_barrier((pair_full, row_grad))
     out_back = first_back[:, :width]
     dot_back = jnp.sum(first_back[:, width:].astype(F32), axis=1)
-    at_slot = place.astype(F32) * dot_back[None, :]
-    gate_grad = jnp.sum(jnp.where(named, at_slot[:, None, :], 0.0), axis=2) / gates
+    at_slot = place.astype(F32) * dot_back[:, None]
+    gate_grad = (jnp.sum(jnp.where(named, at_slot[None], 0.0), axis=1) / gates_by).T
 
     weighted_pair = (slot_share * pair_full.astype(F32)).astype(BF16)
     weighted_hidden = (slot_share * hidden_full.astype(F32)).astype(BF16)
@@ -118,10 +119,14 @@
 
     gate_hi = gate_of.astype(BF16)
     gate_lo = (gate_of - gate_hi.astype(F32)).astype(BF16)
-    combine = jnp.concatenate([gate_hi, gate_lo], axis=0)
-    mixed_parts = jnp.dot(combine, out_back, preferred_element_type=F32)
+    combine = jnp.concatenate([gate_hi, gate_lo], axis=1)
+    mixed_parts = lax.dot_general(
+        combine, out_back, (((0,), (0,)), ((), ())), preferred_element_type=F32
+    )
     mixed = (mixed_parts[:rows] + mixed_parts[rows:]).astype(BF16)
-    token_grad = jnp.dot(place, grad_back, preferred_element_type=F32).astype(BF16)
+    token_grad = lax.dot_general(
+        place, grad_back, (((0,), (0,)), ((), ())), preferred_element_type=F32
+    ).astype(BF16)
     return (mixed, gate_grad, token_grad, weight_grads[None])
 
 

time: 257 us -> 256 us (level)
  local copies, waits for them, and re-layouts: 6.56 us -> 3.97 us
    unnamed x33 -> x26, local copies, waits for them, and re-layouts: 5.28 us -> 2.71 us
where the time goes in v7:
time: 256 us; the launch traced here: 254 us
  waiting for transfers between devices  104 us (41%)
  blocking collectives  91 us (36%)
  starting transfers between devices  18.4 us (7%)
  between operations  14.3 us (6%)
  other arithmetic  11.5 us (4%)
  matrix products  9.97 us (4%)
  local copies, waits for them, and re-layouts  3.97 us (2%)
    reduce_scatter x1, waiting for transfers between devices, shards(): sums = lax.psum_scatter(part, 'dp', scatter_dimension=0, tiled=True)  87.8 us
    all_gather x2, blocking collectives, near(): lax.all_gather(value, 'dp', axis=0, tiled=False, axis_index_groups=nearby)  34.3 us
    all_to_all x1, blocking collectives, shards(): lax.all_to_all(outgoing, 'expert', split_axis=0, concat_axis=0, tiled=True)  33.4 us
    all_gather x1, blocking collectives, shards(): lax.all_gather(payload, 'dp', axis=0, tiled=True, axis_index_groups=strided)  23.3 us
    all_to_all x2, starting transfers between devices, send_back(): lax.all_to_all(sent, 'expert', split_axis=0, concat_axis=0, tiled=True)  18.3 us
    all_to_all x2, waiting for transfers between devices, send_back(): lax.all_to_all(sent, 'expert', split_axis=0, concat_axis=0, tiled=True)  12.4 us
  transfers between devices with their start and end apart: 4, of which 4 were waited for; matrix products, arithmetic and copies ran while one was open for 5% of the time, Pallas kernels for 0%

profile of v7, /device:TPU:6, one launch (start us, length us, event | category | flops | bytes accessed | tf_op | source)
XLA Modules:
  0.0 253.8 jit_solution(4969604722175659045)
XLA Ops:
  7.3 0.9 compare_reduce_fusion
  8.2 0.8 fusion.11
  9.1 0.8 fusion.42
  9.9 0.6 copy-done.5
  10.5 1.1 fusion.4
  11.6 33.4 %all_to_all.15 = bf16[64,8,512]{2,1,0:T(8,128)(2,1)S(1)} all-to-all(bf16[64,8,512]{2,1,0:T(8,128)(2,1)S(1)} %fusion.4), channel_id=1, replica_groups=mesh['dp'=16,'expert'=64] {'expert'}, dimensions={0} | all-to-all | bytes 1048576 | tf_op jit(solution)/shard_map/all_to_all | solution.py:37
  45.0 0.8 fusion.8
  46.2 3.2 %pad_maximum_fusion = f32[512,3,1024]{2,0,1:T(8,128)} fusion(f32[512,1,1024]{2,0,1:T(8,128)S(1)} %convolution_bitcast_fusion, f32[512,2,1024]{2,0,1:T(8,128)S(1)} %fusion.8), kind=kLoop, calls=%fused_computation | loop fusion | flops 1572864 | bytes 12582912 | tf_op jit(solution)/shard_map/concatenate | solution.py:46
  49.5 0.6 copy-done.11
  50.1 0.6 convert_reduce_fusion.1
  50.7 0.6 convert_divide_fusion
  51.8 87.8 %reduce-scatter.2.cloned.1.call-done = f32[32,3,1024]{2,0,1:T(8,128)} async-done(((f32[512,3,1024]{2,0,1:T(8,128)}), f32[32,3,1024]{2,0,1:T(8,128)}) %reduce-scatter.2.cloned.1.call-update) | async-done | bytes 393232 | tf_op jit(solution)/shard_map/reduce_scatter | solution.py:47
  139.6 1.2 fusion.26
  140.8 0.7 pad_maximum_fusion.5
  141.6 23.3 %all_gather.18 = bf16[128,1152]{1,0:T(8,128)(2,1)S(1)} all-gather(bf16[32,1152]{1,0:T(8,128)(2,1)S(1)} %pad_maximum_fusion.6), channel_id=1, replica_groups={{0,256,512,768},{64,320,576,832},{128,384,640,896},{192,448,704,960},{1..., dimensions={0}, use_global_device_ids=true | all-gather | bytes 368640 | tf_op jit(solution)/shard_map/all_gather | solution.py:77
  165.0 18.1 %all-gather.1 = bf16[512,640]{1,0:T(8,128)(2,1)S(1)} all-gather(bf16[128,640]{1,0:T(8,128)(2,1)S(1)} %slice.63), channel_id=3, replica_groups={{0,64,128,192},{256,320,384,448},{512,576,640,704},{768,832,896,960},{1..., dimensions={0}, use_global_device_ids=true | all-gather | bytes 819200 | tf_op jit(solution)/shard_map/all_gather | solution.py:81
  183.2 16.2 %all-gather = bf16[512,512]{1,0:T(8,128)(2,1)S(1)} all-gather(bf16[128,512]{1,0:T(8,128)(2,1)S(1)} %slice.62), channel_id=2, replica_groups={{0,64,128,192},{256,320,384,448},{512,576,640,704},{768,832,896,960},{1..., dimensions={0}, use_global_device_ids=true | all-gather | bytes 655360 | tf_op jit(solution)/shard_map/all_gather | solution.py:81
  199.5 0.8 copy.26
  200.2 0.5 convolution_convert_fusion.4
  201.2 0.9 copy.25
  202.1 11.3 %all-to-all-start.1 = ((bf16[64,8,384]{2,1,0:T(8,128)(2,1)}), bf16[64,8,384]{2,1,0:T(8,128)(2,1)S(1)}, u32[]{:S(2)}, u32[]{:S(2)}) async-start(bf16[64,8,384]{2,1,0:T(8,128)(2,1)} %bitcast.19), calls=%async_computation.2 | async-start | bytes 786432 | tf_op jit(solution)/shard_map/all_to_all | solution.py:94
  213.4 1.4 fusion.3
  214.8 4.2 %all-gather.4.cloned.1.call-done = bf16[512,2048]{1,0:T(8,128)(2,1)} async-done(((bf16[32,2048]{1,0:T(8,128)(2,1)}), bf16[512,2048]{1,0:T(8,128)(2,1)}) %all-gather.4.cloned.1.call-update) | async-done | bytes 2097168 | tf_op jit(solution)/shard_map/all_gather | solution.py:62
  219.0 3.2 %convolution_convert_fusion.3 = bf16[512,256]{1,0:T(8,128)(2,1)} fusion(bf16[512,2048]{1,0:T(8,128)(2,1)} %all-gather.4.cloned.1.call-done, bf16[2048,256]{0,1:T(8,128)(2,1)S(1)} %bitcast.106), kind=kOutput, calls=%fused_computation.14 | convolution fusion | flops 537001984 | bytes 3407872 | tf_op jit(solution)/shard_map/dot_general | solution.py:98
  223.1 0.5 fusion.2
  223.6 4.0 %all-to-all-done.1 = bf16[64,8,384]{2,1,0:T(8,128)(2,1)S(1)} async-done(((bf16[64,8,384]{2,1,0:T(8,128)(2,1)}), bf16[64,8,384]{2,1,0:T(8,128)(2,1)S(1)}, u32[]{:S(2)}, u32[]{:S(2)}) %all-to-all-start.1) | async-done | bytes 393248 | tf_op jit(solution)/shard_map/all_to_all | solution.py:94
  227.5 7.0 %all-to-all-start.2 = ((bf16[64,8,256]{2,1,0:T(8,128)(2,1)}), bf16[64,8,256]{2,1,0:T(8,128)(2,1)S(1)}, u32[]{:S(2)}, u32[]{:S(2)}) async-start(bf16[64,8,256]{2,1,0:T(8,128)(2,1)} %bitcast.22), calls=%async_computation.3 | async-start | bytes 524288 | tf_op jit(solution)/shard_map/all_to_all | solution.py:94
  235.0 0.6 bitcast_divide_fusion
  235.6 1.3 maximum_bitcast_fusion
  237.0 0.6 fusion.37
  237.7 8.5 %all-to-all-done.2 = bf16[64,8,256]{2,1,0:T(8,128)(2,1)S(1)} async-done(((bf16[64,8,256]{2,1,0:T(8,128)(2,1)}), bf16[64,8,256]{2,1,0:T(8,128)(2,1)S(1)}, u32[]{:S(2)}, u32[]{:S(2)}) %all-to-all-start.2) | async-done | bytes 262176 | tf_op jit(solution)/shard_map/all_to_all | solution.py:94
  246.2 0.8 convolution_convert_fusion.5
  (50 shorter events, 3.1 us)
Async XLA Ops:
  7.2 38.6 %copy-start = (bf16[1,256,1024]{2,1,0:T(8,128)(2,1)S(1)}, bf16[1,256,1024]{2,1,0:T(8,128)(2,1)}, u32[]{:S(2)}) copy-start(bf16[1,256,1024]{2,1,0:T(8,128)(2,1)} %param.12) | copy-start | bytes 1572868
  7.2 37.8 %copy-start.1 = (bf16[1,256,2,1024]{3,2,1,0:T(2,128)(2,1)S(1)}, bf16[1,256,2,1024]{3,2,1,0:T(2,128)(2,1)}, u32[]{:S(2)}) copy-start(bf16[1,256,2,1024]{3,2,1,0:T(2,128)(2,1)} %param.11) | copy-start | bytes 3145732
  7.2 132.4 %reduce-scatter.2.cloned.1.call-start = ((), (), s32[]{:S(2)}) async-start(), calls=%async_computation.4 | async-start | bytes 6684672 | tf_op jit(solution)/shard_map/reduce_scatter | solution.py:47
  9.9 0.6 copy-start.5
  49.4 0.7 copy-start.11
  49.5 169.5 %all-gather.4.cloned.1.call-start = ((), (), s32[]{:S(2)}) async-start(), calls=%async_computation.5 | async-start | bytes 2228224 | tf_op jit(solution)/shard_map/all_gather | solution.py:62
  200.2 0.9 copy-start.3
  202.1 25.4 %all-to-all-start.1 = ((bf16[64,8,384]{2,1,0:T(8,128)(2,1)}), bf16[64,8,384]{2,1,0:T(8,128)(2,1)S(1)}, u32[]{:S(2)}, u32[]{:S(2)}) async-start(bf16[64,8,384]{2,1,0:T(8,128)(2,1)} %bitcast.19), calls=%async_computation.2 | async-start | bytes 786432 | tf_op jit(solution)/shard_map/all_to_all | solution.py:94
  219.0 3.2 %copy-start.2 = (bf16[512,2048]{1,0:T(8,128)(2,1)S(1)}, bf16[512,2048]{1,0:T(8,128)(2,1)}, u32[]{:S(2)}) copy-start(bf16[512,2048]{1,0:T(8,128)(2,1)} %all-gather.4.cloned.1.call-done) | copy-start | bytes 6291460
  222.6 12.1 %copy-start.6 = (bf16[512,32]{0,1:T(8,128)(2,1)S(1)}, bf16[512,32]{0,1:T(8,128)(2,1)}, u32[]{:S(2)}) copy-start(bf16[512,32]{0,1:T(8,128)(2,1)} %copy-done.5) | copy-start | bytes 98308
  222.6 12.2 %copy-start.7 = (s32[32,8]{0,1:T(8,128)S(1)}, s32[32,8]{0,1:T(8,128)}, u32[]{:S(2)}) copy-start(s32[32,8]{0,1:T(8,128)} %param.8) | copy-start | bytes 3076
  222.6 12.3 %copy-start.10 = (f32[32,8]{0,1:T(8,128)S(1)}, f32[32,8]{0,1:T(8,128)}, u32[]{:S(2)}) copy-start(f32[32,8]{0,1:T(8,128)} %param.9) | copy-start | bytes 3076
  222.6 12.9 %copy-start.4 = (bf16[256,1,1024]{2,0,1:T(8,128)(2,1)S(1)}, bf16[256,1,1024]{2,0,1:T(8,128)(2,1)}, u32[]{:S(2)}) copy-start(bf16[256,1,1024]{2,0,1:T(8,128)(2,1)} %fusion.3) | copy-start | bytes 1572868
  223.6 13.3 %copy-start.8 = (bf16[512,32]{0,1:T(8,128)(2,1)S(1)}, bf16[512,32]{0,1:T(8,128)(2,1)}, u32[]{:S(2)}) copy-start(bf16[512,32]{0,1:T(8,128)(2,1)} %get-tuple-element.22) | copy-start | bytes 98308
  223.6 13.3 %copy-start.9 = (bf16[512,32]{0,1:T(8,128)(2,1)S(1)}, bf16[512,32]{0,1:T(8,128)(2,1)}, u32[]{:S(2)}) copy-start(bf16[512,32]{0,1:T(8,128)(2,1)} %get-tuple-element.23) | copy-start | bytes 98308
  227.5 18.6 %all-to-all-start.2 = ((bf16[64,8,256]{2,1,0:T(8,128)(2,1)}), bf16[64,8,256]{2,1,0:T(8,128)(2,1)S(1)}, u32[]{:S(2)}, u32[]{:S(2)}) async-start(bf16[64,8,256]{2,1,0:T(8,128)(2,1)} %bitcast.22), calls=%async_computation.3 | async-start | bytes 524288 | tf_op jit(solution)/shard_map/all_to_all | solution.py:94
Sparse Core Ops, SparseCore 0:
  49.6 89.9 reduce-scatter.1
  142.2 76.6 all-gather.3

commit v8 on v7

--- a/solution.py
+++ b/solution.py
@@ -45,11 +45,22 @@
     hidden_grad_part = jnp.dot(grad_rows, down_weight, preferred_element_type=F32)
     part = jnp.concatenate([pair_part, hidden_grad_part[:, None, :]], axis=1)
     sums = lax.psum_scatter(part, "dp", scatter_dimension=0, tiled=True)
-    later_weight, later_counts, _ = lax.optimization_barrier((pair_weight, counts, part))
+    later_weight, later_counts, later_down, _ = lax.optimization_barrier(
+        (pair_weight, counts, down_weight, part)
+    )
+    through = jnp.concatenate(
+        [
+            jnp.pad(later_down, ((0, 0), (0, 128))),
+            jnp.pad(jnp.eye(128, dtype=BF16), ((0, 0), (ff, 0))),
+        ],
+        axis=0,
+    )
     flat_weight = later_weight.reshape(width, 2 * ff).T
     shares = later_counts.astype(F32) / jnp.sum(later_counts.astype(F32))
     slot_share = jnp.repeat(shares, cap)[:, None]
-    sums, flat_weight, slot_share = lax.optimization_barrier((sums, flat_weight, slot_share))
+    sums, flat_weight, slot_share, through = lax.optimization_barrier(
+        (sums, flat_weight, slot_share, through)
+    )
     gate_part, up_part, hidden_grad = sums[:, 0], sums[:, 1], sums[:, 2]
     sig_gate = jax.nn.sigmoid(gate_part)
     silu_gate = gate_part * sig_gate
@@ -84,9 +95,10 @@
 
     low = near(columns[:, :cut])
     high = near(columns[:, cut:])
-    hidden_full = jnp.concatenate([low, high[:, : ff - cut]], axis=1)
+    hidden_dots = jnp.concatenate([low, high], axis=1)
+    hidden_full = hidden_dots[:, :ff]
     expert_out = lax.dot_general(
-        hidden_full, down_weight, (((1,), (1,)), ((), ())), preferred_element_type=F32
+        hidden_dots, through, (((1,), (1,)), ((), ())), preferred_element_type=F32
     ).astype(BF16)
 
     def send_back(value):
@@ -94,7 +106,7 @@
         came = lax.all_to_all(sent, "expert", split_axis=0, concat_axis=0, tiled=True)
         return came.reshape(slots, value.shape[1])
 
-    first_back = send_back(jnp.concatenate([expert_out, high[:, ff - cut :]], axis=1))
+    first_back = send_back(expert_out)
     row_grad = jnp.dot(pair_full, flat_weight, preferred_element_type=F32).astype(BF16)
     grad_back = send_back(row_grad)
     first_back, _ = lax.optimization_barrier((first_back, row_grad))

time: 256 us -> 254 us (level)
  no operation moved by 1% of the time
where the time goes in v8:
time: 254 us; the launch traced here: 252 us
  waiting for transfers between devices  103 us (41%)
  blocking collectives  90.8 us (36%)
  starting transfers between devices  18.3 us (7%)
  between operations  14.3 us (6%)
  other arithmetic  11.6 us (5%)
  matrix products  11.5 us (5%)
    reduce_scatter x1, waiting for transfers between devices, shards(): sums = lax.psum_scatter(part, 'dp', scatter_dimension=0, tiled=True)  87.7 us
    all_gather x2, blocking collectives, near(): lax.all_gather(value, 'dp', axis=0, tiled=False, axis_index_groups=nearby)  34.2 us
    all_to_all x1, blocking collectives, shards(): lax.all_to_all(outgoing, 'expert', split_axis=0, concat_axis=0, tiled=True)  33.4 us
    all_gather x1, blocking collectives, shards(): lax.all_gather(payload, 'dp', axis=0, tiled=True, axis_index_groups=strided)  23.1 us
    all_to_all x2, starting transfers between devices, send_back(): lax.all_to_all(sent, 'expert', split_axis=0, concat_axis=0, tiled=True)  18.2 us
    all_to_all x2, waiting for transfers between devices, send_back(): lax.all_to_all(sent, 'expert', split_axis=0, concat_axis=0, tiled=True)  11.3 us
  transfers between devices with their start and end apart: 4, of which 4 were waited for; matrix products, arithmetic and copies ran while one was open for 5% of the time, Pallas kernels for 0%

profile of v8, /device:TPU:6, one launch (start us, length us, event | category | flops | bytes accessed | tf_op | source)
XLA Modules:
  0.0 252.0 jit_solution(4737083754908989586)
XLA Ops:
  7.3 0.9 compare_reduce_fusion
  8.2 0.8 fusion.20
  9.2 1.1 fusion.5
  10.3 33.4 %all_to_all.15 = bf16[64,8,512]{2,1,0:T(8,128)(2,1)S(1)} all-to-all(bf16[64,8,512]{2,1,0:T(8,128)(2,1)S(1)} %fusion.5), channel_id=1, replica_groups=mesh['dp'=16,'expert'=64] {'expert'}, dimensions={0} | all-to-all | bytes 1048576 | tf_op jit(solution)/shard_map/all_to_all | solution.py:37
  43.7 0.8 fusion.16
  44.7 0.4 convolution_bitcast_fusion
  45.2 3.2 %pad_maximum_fusion = f32[512,3,1024]{2,0,1:T(8,128)} fusion(f32[512,1,1024]{2,0,1:T(8,128)S(1)} %convolution_bitcast_fusion, f32[512,2,1024]{2,0,1:T(8,128)S(1)} %fusion.16), kind=kLoop, calls=%fused_computation | loop fusion | flops 1572864 | bytes 12582912 | tf_op jit(solution)/shard_map/concatenate | solution.py:46
  48.5 0.5 copy-done.7
  49.1 0.6 convert_reduce_fusion.1
  49.7 0.6 convert_divide_fusion
  50.8 87.7 %reduce-scatter.2.cloned.1.call-done = f32[32,3,1024]{2,0,1:T(8,128)} async-done(((f32[512,3,1024]{2,0,1:T(8,128)}), f32[32,3,1024]{2,0,1:T(8,128)}) %reduce-scatter.2.cloned.1.call-update) | async-done | bytes 393232 | tf_op jit(solution)/shard_map/reduce_scatter | solution.py:47
  138.5 1.2 fusion.33
  139.7 0.7 pad_maximum_fusion.1
  140.5 23.1 %all_gather.18 = bf16[128,1152]{1,0:T(8,128)(2,1)S(1)} all-gather(bf16[32,1152]{1,0:T(8,128)(2,1)S(1)} %pad_maximum_fusion.2), channel_id=1, replica_groups={{0,256,512,768},{64,320,576,832},{128,384,640,896},{192,448,704,960},{1..., dimensions={0}, use_global_device_ids=true | all-gather | bytes 368640 | tf_op jit(solution)/shard_map/all_gather | solution.py:88
  163.7 17.5 %all-gather.1 = bf16[512,640]{1,0:T(8,128)(2,1)S(1)} all-gather(bf16[128,640]{1,0:T(8,128)(2,1)S(1)} %slice.59), channel_id=3, replica_groups={{0,64,128,192},{256,320,384,448},{512,576,640,704},{768,832,896,960},{1..., dimensions={0}, use_global_device_ids=true | all-gather | bytes 819200 | tf_op jit(solution)/shard_map/all_gather | solution.py:92
  181.2 16.8 %all-gather = bf16[512,512]{1,0:T(8,128)(2,1)S(1)} all-gather(bf16[128,512]{1,0:T(8,128)(2,1)S(1)} %slice.58), channel_id=2, replica_groups={{0,64,128,192},{256,320,384,448},{512,576,640,704},{768,832,896,960},{1..., dimensions={0}, use_global_device_ids=true | all-gather | bytes 655360 | tf_op jit(solution)/shard_map/all_gather | solution.py:92
  198.1 0.8 copy-done.3
  198.9 1.6 fusion.6
  200.4 10.9 %all-to-all-start.1 = ((bf16[64,8,384]{2,1,0:T(8,128)(2,1)}), bf16[64,8,384]{2,1,0:T(8,128)(2,1)S(1)}, u32[]{:S(2)}, u32[]{:S(2)}) async-start(bf16[64,8,384]{2,1,0:T(8,128)(2,1)} %fusion.6), calls=%async_computation.2 | async-start | bytes 786432 | tf_op jit(solution)/shard_map/all_to_all | solution.py:106
  211.3 2.4 fusion.4
  213.8 4.4 %all-gather.4.cloned.1.call-done = bf16[512,2048]{1,0:T(8,128)(2,1)} async-done(((bf16[32,2048]{1,0:T(8,128)(2,1)}), bf16[512,2048]{1,0:T(8,128)(2,1)}) %all-gather.4.cloned.1.call-update) | async-done | bytes 2097168 | tf_op jit(solution)/shard_map/all_gather | solution.py:73
  218.1 3.2 %convolution_convert_fusion.4 = bf16[512,256]{1,0:T(8,128)(2,1)} fusion(bf16[512,2048]{1,0:T(8,128)(2,1)} %all-gather.4.cloned.1.call-done, bf16[2048,256]{0,1:T(8,128)(2,1)S(1)} %bitcast.105), kind=kOutput, calls=%fused_computation.18 | convolution fusion | flops 537001984 | bytes 3407872 | tf_op jit(solution)/shard_map/dot_general | solution.py:110
  221.3 0.4 multiply_convert_fusion
  221.8 0.5 fusion.2
  222.2 0.5 fusion.3
  222.7 2.8 %all-to-all-done.1 = bf16[64,8,384]{2,1,0:T(8,128)(2,1)S(1)} async-done(((bf16[64,8,384]{2,1,0:T(8,128)(2,1)}), bf16[64,8,384]{2,1,0:T(8,128)(2,1)S(1)}, u32[]{:S(2)}, u32[]{:S(2)}) %all-to-all-start.1) | async-done | bytes 393248 | tf_op jit(solution)/shard_map/all_to_all | solution.py:106
  225.5 7.3 %all-to-all-start.2 = ((bf16[64,8,256]{2,1,0:T(8,128)(2,1)}), bf16[64,8,256]{2,1,0:T(8,128)(2,1)S(1)}, u32[]{:S(2)}, u32[]{:S(2)}) async-start(bf16[64,8,256]{2,1,0:T(8,128)(2,1)} %bitcast.21), calls=%async_computation.3 | async-start | bytes 524288 | tf_op jit(solution)/shard_map/all_to_all | solution.py:106
  233.2 0.6 bitcast_divide_fusion
  233.8 1.3 maximum_bitcast_fusion
  235.3 0.6 fusion.44
  235.9 8.5 %all-to-all-done.2 = bf16[64,8,256]{2,1,0:T(8,128)(2,1)S(1)} async-done(((bf16[64,8,256]{2,1,0:T(8,128)(2,1)}), bf16[64,8,256]{2,1,0:T(8,128)(2,1)S(1)}, u32[]{:S(2)}, u32[]{:S(2)}) %all-to-all-start.2) | async-done | bytes 262176 | tf_op jit(solution)/shard_map/all_to_all | solution.py:106
  244.4 0.8 convolution_convert_fusion.5
  (40 shorter events, 1.9 us)
Async XLA Ops:
  7.2 36.5 %copy-start = (bf16[1,256,2,1024]{3,2,1,0:T(2,128)(2,1)S(1)}, bf16[1,256,2,1024]{3,2,1,0:T(2,128)(2,1)}, u32[]{:S(2)}) copy-start(bf16[1,256,2,1024]{3,2,1,0:T(2,128)(2,1)} %param.11) | copy-start | bytes 3145732
  7.2 131.3 %reduce-scatter.2.cloned.1.call-start = ((), (), s32[]{:S(2)}) async-start(), calls=%async_computation.4 | async-start | bytes 6684672 | tf_op jit(solution)/shard_map/reduce_scatter | solution.py:47
  43.7 1.0 copy-start.2
  48.4 0.7 copy-start.7
  48.4 169.7 %all-gather.4.cloned.1.call-start = ((), (), s32[]{:S(2)}) async-start(), calls=%async_computation.5 | async-start | bytes 2228224 | tf_op jit(solution)/shard_map/all_gather | solution.py:73
  198.1 0.8 copy-start.3
  200.4 25.1 %all-to-all-start.1 = ((bf16[64,8,384]{2,1,0:T(8,128)(2,1)}), bf16[64,8,384]{2,1,0:T(8,128)(2,1)S(1)}, u32[]{:S(2)}, u32[]{:S(2)}) async-start(bf16[64,8,384]{2,1,0:T(8,128)(2,1)} %fusion.6), calls=%async_computation.2 | async-start | bytes 786432 | tf_op jit(solution)/shard_map/all_to_all | solution.py:106
  218.1 3.2 %copy-start.1 = (bf16[512,2048]{1,0:T(8,128)(2,1)S(1)}, bf16[512,2048]{1,0:T(8,128)(2,1)}, u32[]{:S(2)}) copy-start(bf16[512,2048]{1,0:T(8,128)(2,1)} %all-gather.4.cloned.1.call-done) | copy-start | bytes 6291460
  221.7 11.2 %copy-start.5 = (s32[32,8]{0,1:T(8,128)S(1)}, s32[32,8]{0,1:T(8,128)}, u32[]{:S(2)}) copy-start(s32[32,8]{0,1:T(8,128)} %param.8) | copy-start | bytes 3076
  221.7 11.4 %copy-start.6 = (f32[32,8]{0,1:T(8,128)S(1)}, f32[32,8]{0,1:T(8,128)}, u32[]{:S(2)}) copy-start(f32[32,8]{0,1:T(8,128)} %param.9) | copy-start | bytes 3076
  221.8 12.0 %copy-start.4 = (bf16[256,1,1024]{2,0,1:T(8,128)(2,1)S(1)}, bf16[256,1,1024]{2,0,1:T(8,128)(2,1)}, u32[]{:S(2)}) copy-start(bf16[256,1,1024]{2,0,1:T(8,128)(2,1)} %fusion.4) | copy-start | bytes 1572868
  225.5 18.9 %all-to-all-start.2 = ((bf16[64,8,256]{2,1,0:T(8,128)(2,1)}), bf16[64,8,256]{2,1,0:T(8,128)(2,1)S(1)}, u32[]{:S(2)}, u32[]{:S(2)}) async-start(bf16[64,8,256]{2,1,0:T(8,128)(2,1)} %bitcast.21), calls=%async_computation.3 | async-start | bytes 524288 | tf_op jit(solution)/shard_map/all_to_all | solution.py:106
Sparse Core Ops, SparseCore 0:
  48.6 89.9 reduce-scatter.1
  141.2 76.8 all-gather.3
